TPU v7x, 32 devices: a whole 2x2x4 slice. The times are simulated.
32 devices in a mesh: dp: 16 (over z, x, core), mp: 2 (over y).
Axes of the slice: x: 2, y: 2, z: 4, core: 2. Of those that a mesh axis runs over, the one named last changes fastest.
Arguments:
- inputs: bfloat16 [16, 2048, 768], P('dp', 'mp'), may hold values from -6 to 6
- seg_ids: int32 [16, 2048], P('dp'), may hold values from 0 to 7, as said below
- omega: float32 [64, 32], replicated, may hold values from -5 to 5
- norm1_gain: float32 [768], replicated, may hold values from 0.1 to 1.9
- qkv_weight: bfloat16 [768, 3, 768], P(None, None, 'mp'), may hold values from -0.21875 to 0.21875
- out_weight: bfloat16 [768, 768], P('mp'), may hold values from -3.5 to 3.5
- norm2_gain: float32 [768], replicated, may hold values from 0.1 to 1.9
- up_weight: bfloat16 [768, 3072], P(None, 'mp'), may hold values from -0.21875 to 0.21875
- down_weight: bfloat16 [3072, 768], P('mp'), may hold values from -0.109375 to 0.109375
- out_grad: bfloat16 [16, 2048, 768], P('dp', 'mp'), may hold values from -6 to 6
Outputs:
- output: bfloat16 [16, 2048, 768], P('dp', 'mp')
- input_grad: float32 [16, 2048, 768], P('dp', 'mp')
- norm1_gain_grad: float32 [768], P(('dp', 'mp'))
- qkv_weight_grad: float32 [768, 3, 768], P('dp', None, 'mp')
- out_weight_grad: float32 [768, 768], P('mp', 'dp')
- norm2_gain_grad: float32 [768], P(('dp', 'mp'))
- up_weight_grad: float32 [768, 3072], P('dp', 'mp')
- down_weight_grad: float32 [3072, 768], P('mp', 'dp')
Inputs may be any that keep to these rules, and one draw needn't show every extreme that they name: `seg_ids`: along each sequence the document number never falls, starts at 0 and ends at 7; no document boundary lies in the middle half of a sequence.
All inputs are finite; a program needn't handle non-finite values.
Results may differ from a plain program's by a relative error of at most 0.0095.
Values may be sent and summed in bfloat16 or wider, within the bound.
No kernel may reach another device: no remote copies, remote signals or barrier semaphores. Data moves between devices by JAX's collectives and lax.ppermute only.
A program may use at most 192 MiB of HBM per device.

v0:
```python
import jax
import jax.numpy as jnp
from jax import lax
from jax.sharding import PartitionSpec as P

SEGS = 8


HIGH = lax.Precision.HIGHEST


def layer_norm(values, gain):
    middle = jnp.mean(values, axis=-1, keepdims=True)
    centred = values - middle
    spread = jnp.mean(centred * centred, axis=-1, keepdims=True)
    return centred * lax.rsqrt(spread + 1e-05) * gain


def rotary_tables(total, head_size):
    places = jnp.arange(total).astype(jnp.float32)
    rates = 10000.0 ** (-(jnp.arange(head_size // 2).astype(jnp.float32) * 2.0 / head_size))
    angles = places[:, None] * rates[None, :]
    return (jnp.cos(angles)[:, None, :], jnp.sin(angles)[:, None, :])


def rotate(vectors, cosine, sine_table):
    half = vectors.shape[-1] // 2
    first = vectors[..., :half]
    second = vectors[..., half:]
    return jnp.concatenate(
        [first * cosine - second * sine_table, second * cosine + first * sine_table], axis=-1
    )


def features(vectors, omega, cosine, sine_table):
    scale = omega.shape[0] ** (-0.25)
    turned = rotate(vectors, cosine, sine_table) * scale
    return jax.nn.softplus(jnp.einsum("lhd,df->lhf", turned, omega, precision=HIGH))


def attend(qkv, onehot, omega, cosine, sine_table):
    total = qkv.shape[0]
    head_size = omega.shape[0]
    parts = qkv.reshape(total, 3, -1, head_size)
    query_feat = features(parts[:, 0], omega, cosine, sine_table)
    key_feat = features(parts[:, 1], omega, cosine, sine_table)
    values = parts[:, 2]
    key_doc = onehot[:, :, None, None] * key_feat[:, None]
    state = jnp.einsum("lshf,lhe->hsfe", key_doc, values, precision=HIGH)
    totals = jnp.einsum("ls,lhf->hsf", onehot, key_feat, precision=HIGH)
    query_doc = onehot[:, :, None, None] * query_feat[:, None]
    numer = jnp.einsum("lshf,hsfe->lhe", query_doc, state, precision=HIGH)
    denom = jnp.einsum("lshf,hsf->lh", query_doc, totals, precision=HIGH)
    return (numer / denom[:, :, None]).reshape(total, -1)


def matmul(left, right):
    return jnp.dot(left, right, preferred_element_type=jnp.float32)


def times_transpose(left, right):
    return lax.dot_general(
        left, right, (((1,), (1,)), ((), ())), preferred_element_type=jnp.float32
    )


def transpose_times(left, right):
    return lax.dot_general(
        left, right, (((0,), (0,)), ((), ())), preferred_element_type=jnp.float32
    )


def settle_ffn(down_grad, up_grad):
    return (down_grad, up_grad)


def settle_attn(qkv_grad, out_grad_w):
    return (qkv_grad, out_grad_w)


def heads_pass(
    inputs,
    onehot,
    omega,
    norm1_gain,
    qkv_weight,
    out_weight,
    norm2_gain,
    up_weight,
    down_weight,
    out_grad,
):
    width = inputs.shape[2]
    total = onehot.shape[0]
    rows_in = inputs[0].astype(jnp.float32)
    cosine, sine_table = rotary_tables(total, omega.shape[0])
    wqkv = qkv_weight.reshape(width, -1)

    def attention_core(qkv):
        return attend(qkv, onehot, omega, cosine, sine_table)

    first = layer_norm(rows_in, norm1_gain).astype(jnp.bfloat16)
    first_full = lax.all_gather(first, "mp", axis=0, tiled=True)
    qkv = matmul(first_full, wqkv)
    attn_f, core_back = jax.vjp(attention_core, qkv)
    attn = attn_f.astype(jnp.bfloat16)
    branch = lax.psum_scatter(matmul(attn, out_weight), "mp", scatter_dimension=0, tiled=True)
    middle = rows_in + branch
    second = layer_norm(middle, norm2_gain).astype(jnp.bfloat16)
    second_full = lax.all_gather(second, "mp", axis=0, tiled=True)
    hpre = matmul(second_full, up_weight)
    hact_f, gelu_back = jax.vjp(jax.nn.gelu, hpre)
    hact = hact_f.astype(jnp.bfloat16)
    ffn = lax.psum_scatter(
        matmul(hact, down_weight).astype(jnp.bfloat16), "mp", scatter_dimension=0, tiled=True
    ).astype(jnp.float32)
    output = (middle + ffn).astype(jnp.bfloat16)[None]
    cotangent = out_grad[0]
    cotangent_full = lax.all_gather(cotangent, "mp", axis=0, tiled=True)
    dhact = times_transpose(cotangent_full, down_weight)
    dhpre = gelu_back(dhact)[0].astype(jnp.bfloat16)
    down_grad = transpose_times(hact, cotangent_full)
    up_grad = transpose_times(second_full, dhpre)
    down_grad, up_grad = settle_ffn(down_grad, up_grad)
    dsecond = lax.psum_scatter(
        times_transpose(dhpre, up_weight), "mp", scatter_dimension=0, tiled=True
    )
    _, second_back = jax.vjp(layer_norm, middle, norm2_gain)
    dmiddle_part, gain_two_grad = second_back(dsecond)
    dmiddle = cotangent.astype(jnp.float32) + dmiddle_part
    dbranch = dmiddle.astype(jnp.bfloat16)
    dbranch_full = lax.all_gather(dbranch, "mp", axis=0, tiled=True)
    out_grad_w = transpose_times(attn, dbranch_full)
    dattn = times_transpose(dbranch_full, out_weight)
    dqkv = core_back(dattn)[0].astype(jnp.bfloat16)
    qkv_grad = transpose_times(first_full, dqkv).reshape(qkv_weight.shape)
    dfirst = lax.psum_scatter(
        times_transpose(dqkv, wqkv).astype(jnp.bfloat16), "mp", scatter_dimension=0, tiled=True
    ).astype(jnp.float32)
    _, first_back = jax.vjp(layer_norm, rows_in, norm1_gain)
    dinput_part, gain_one_grad = first_back(dfirst)
    input_grad = (dmiddle + dinput_part)[None]
    return (
        output,
        input_grad,
        gain_one_grad,
        qkv_grad,
        out_grad_w,
        gain_two_grad,
        up_grad,
        down_grad,
    )


def on_device(
    inputs,
    seg_ids,
    omega,
    norm1_gain,
    qkv_weight,
    out_weight,
    norm2_gain,
    up_weight,
    down_weight,
    out_grad,
):
    onehot = (seg_ids[0][:, None] == jnp.arange(SEGS)[None, :]).astype(jnp.float32)
    results = heads_pass(
        inputs,
        onehot,
        omega,
        norm1_gain,
        qkv_weight,
        out_weight,
        norm2_gain,
        up_weight,
        down_weight,
        out_grad,
    )
    output, input_grad, gain_one_grad, qkv_grad, out_grad_w, gain_two_grad, up_sum, down_sum = (
        results
    )
    qkv_grad, out_grad_w = settle_attn(qkv_grad, out_grad_w)
    qkv_sum, out_sum, up_sum, down_sum = (
        lax.psum_scatter(qkv_grad, "dp", scatter_dimension=0, tiled=True),
        lax.psum_scatter(out_grad_w, "dp", scatter_dimension=1, tiled=True),
        lax.psum_scatter(up_sum, "dp", scatter_dimension=0, tiled=True),
        lax.psum_scatter(down_sum, "dp", scatter_dimension=1, tiled=True),
    )
    gain_one_sum, gain_two_sum = (
        lax.psum_scatter(gain_one_grad, ("dp", "mp"), scatter_dimension=0, tiled=True),
        lax.psum_scatter(gain_two_grad, ("dp", "mp"), scatter_dimension=0, tiled=True),
    )
    return (output, input_grad, gain_one_sum, qkv_sum, out_sum, gain_two_sum, up_sum, down_sum)


def solution(mesh):
    return jax.shard_map(
        on_device,
        mesh=mesh,
        in_specs=(
            P("dp", "mp", None),
            P("dp", None),
            P(),
            P(),
            P(None, None, "mp"),
            P("mp", None),
            P(),
            P(None, "mp"),
            P("mp", None),
            P("dp", "mp", None),
        ),
        out_specs=(
            P("dp", "mp", None),
            P("dp", "mp", None),
            P(("dp", "mp")),
            P("dp", None, "mp"),
            P("mp", "dp"),
            P(("dp", "mp")),
            P("dp", "mp"),
            P("mp", "dp"),
        ),
        check_vma=False,
    )
```

profile of v0, /device:TPU:0, one launch (start us, length us, event | category | flops | bytes accessed | tf_op | source)
XLA Modules:
  0.0 929.4 jit_solution(8513068313170204244)
XLA Ops:
  7.3 1.8 convert_reduce_fusion
  9.1 2.0 fusion.41
  12.3 1.7 fusion.40
  14.1 3.8 copy.25
  18.0 1.0 multiply_cosine_fusion
  19.0 42.8 %all-gather.6.cloned.1.call-done = bf16[2048,768]{1,0:T(8,128)(2,1)} async-done(((bf16[1024,768]{1,0:T(8,128)(2,1)}), bf16[2048,768]{1,0:T(8,128)(2,1)}) %all-gather.6.cloned.1.call-update) | async-done | bytes 3145744 | tf_op jit(solution)/shard_map/all_gather | solution.py:103
  61.8 6.3 fusion.50
  69.0 1.4 multiply_subtract_fusion
  70.4 3.0 fusion.78
  73.4 2.3 fusion.84
  75.7 0.9 add_select_fusion
  76.6 4.2 compare_select_fusion
  80.8 7.8 fusion.4
  88.7 11.1 %fusion.10 = f32[6,8,32,64]{3,2,1,0:T(8,128)S(1)} fusion(f32[2048,6,32]{0,2,1:T(8,128)S(1)} %add_select_fusion, f32[2048,8]{0,1:T(8,128)S(1)} %fusion.82, f32[2048,3,6,64]{0,3,2,1:T(8,128)S(1)} %fusion.50), kind=kOutput, calls=%fused_computation.12 | convolution fusion | flops 2419064832 | bytes 5177344 | tf_op jit(solution)/shard_map/jvp(lshf,lhe->hsfe)/dot_general | solution.py:49
  99.8 10.1 %fusion.56 = (bf16[2048,6,64]{0,2,1:T(8,128)(2,1)S(1)}, f32[6,64,2048,1]{2,1,3,0:T(8,128)}) fusion(f32[2048,6]{0,1:T(8,128)S(1)} %bitcast.187, f32[6,8,32,64]{3,2,1,0:T(8,128)S(1)} %fusion.10, f32[2048,6,32]{0,2,1:T(8,128)S(1)} %get-tuple-element.50, f32[2048,8]{0,1:T(8,128)S(1)} %fusion.82), kind=kOutput, calls=%fused_computation.80 | convolution fusion | flops 2420637696 | bytes 6799360 | tf_op jit(solution)/shard_map/jvp(lshf,hsfe->lhe)/dot_general | solution.py:52
  109.8 1.1 copy-done.12
  111.0 4.5 fusion.103
  115.6 77.2 %reduce-scatter.9.cloned.1.call-done = f32[1024,768]{1,0:T(8,128)} async-done(((f32[2048,768]{1,0:T(8,128)}), f32[1024,768]{1,0:T(8,128)}) %reduce-scatter.9.cloned.1.call-update) | async-done | bytes 3145744 | tf_op jit(solution)/shard_map/reduce_scatter | solution.py:107
  192.7 2.7 fusion.101
  196.0 1.2 copy-done.2
  197.1 1.6 multiply_convert_fusion.1
  199.4 44.5 %all-gather.8.cloned.1.call-done = bf16[2048,768]{1,0:T(8,128)(2,1)} async-done(((bf16[1024,768]{1,0:T(8,128)(2,1)}), bf16[2048,768]{1,0:T(8,128)(2,1)}) %all-gather.8.cloned.1.call-update) | async-done | bytes 3145744 | tf_op jit(solution)/shard_map/all_gather | solution.py:110
  243.9 10.1 %fusion.104 = f32[2048,1536]{1,0:T(8,128)} fusion(bf16[2048,768]{1,0:T(8,128)(2,1)} %all-gather.8.cloned.1.call-done, bf16[768,1536]{1,0:T(8,128)(2,1)S(1)} %copy-done), kind=kOutput, calls=%fused_computation.171 | convolution fusion | flops 4831838208 | bytes 18087936 | tf_op jit(solution)/shard_map/dot_general | solution.py:58
  254.0 36.3 %all-gather.12.cloned.1.call-done = bf16[1,2048,768]{2,1,0:T(8,128)(2,1)} async-done(((bf16[1,1024,768]{2,1,0:T(8,128)(2,1)}), bf16[1,2048,768]{2,1,0:T(8,128)(2,1)}) %all-gather.12.cloned.1.call-update) | async-done | bytes 3145744 | tf_op jit(solution)/shard_map/all_gather | solution.py:119
  290.3 15.7 %fusion.18 = bf16[2048,1536]{1,0:T(8,128)(2,1)S(1)} fusion(f32[2048,1536]{1,0:T(8,128)} %fusion.104, bf16[1536,768]{1,0:T(8,128)(2,1)} %param.19, bf16[1,2048,768]{2,1,0:T(8,128)(2,1)} %all-gather.12.cloned.1.call-done), kind=kOutput, calls=%fused_computation.20 | convolution fusion | flops 4894752768 | bytes 24379392 | tf_op jit(solution)/shard_map/dot_general | solution.py:62
  306.0 2.7 copy-done.47
  308.7 6.9 fusion.105
  315.7 1.6 copy-done.42
  317.3 11.7 %convolution_convert_fusion.1 = bf16[2048,768]{1,0:T(8,128)(2,1)} fusion(bf16[1536,768]{1,0:T(8,128)(2,1)S(1)} %copy-done.42, f32[2048,1536]{1,0:T(8,128)} %fusion.104), kind=kOutput, calls=%fused_computation.55 | convolution fusion | flops 4861722624 | bytes 18087936 | tf_op jit(solution)/shard_map/dot_general | solution.py:58
  329.0 63.8 %reduce-scatter.13.cloned.1.call-done = f32[1024,768]{1,0:T(8,128)} async-done(((f32[2048,768]{1,0:T(8,128)}), f32[1024,768]{1,0:T(8,128)}) %reduce-scatter.13.cloned.1.call-update) | async-done | bytes 3145744 | tf_op jit(solution)/shard_map/reduce_scatter | solution.py:125
  392.8 3.4 multiply_reduce_fusion.1
  396.9 41.4 %reduce-scatter.11.cloned.1.call-done = bf16[1024,768]{1,0:T(8,128)(2,1)} async-done(((bf16[2048,768]{1,0:T(8,128)(2,1)}), bf16[1024,768]{1,0:T(8,128)(2,1)}) %reduce-scatter.11.cloned.1.call-update) | async-done | bytes 1572880 | tf_op jit(solution)/shard_map/reduce_scatter | solution.py:114
  438.3 4.9 fusion.100
  443.2 3.6 fusion.66
  447.3 1.2 fusion.79
  449.8 42.0 %all-gather.10.cloned.1.call-done = bf16[2048,768]{1,0:T(8,128)(2,1)} async-done(((bf16[1024,768]{1,0:T(8,128)(2,1)}), bf16[2048,768]{1,0:T(8,128)(2,1)}) %all-gather.10.cloned.1.call-update) | async-done | bytes 3145744 | tf_op jit(solution)/shard_map/all_gather | solution.py:132
  491.9 3.5 fusion.106
  495.5 11.4 %fusion.2 = f32[6,8,32,64]{3,2,1,0:T(8,128)S(1)} fusion(f32[2048,6,32]{0,2,1:T(8,128)S(1)} %copy-done.46, f32[2048,8]{0,1:T(8,128)S(1)} %copy-done.33, f32[2048,6,64]{0,2,1:T(8,128)S(1)} %bitcast.180, f32[2048,6]{0,1:T(8,128)S(1)} %bitcast.188), kind=kOutput, calls=%fused_computation.2 | convolution fusion | flops 2419851264 | bytes 5226496 | tf_op jit(solution)/shard_map/transpose(jvp(lshf,hsfe->lhe))/dot_general | solution.py:52
  506.8 12.1 %fusion.19 = f32[2048,6,32]{0,2,1:T(8,128)S(1)} fusion(f32[2048,8]{0,1:T(8,128)S(1)} %copy-done.33, f32[6,8,32,64]{3,2,1,0:T(8,128)S(1)} %fusion.2, f32[2048,3,6,64]{0,3,2,1:T(8,128)} %copy-done.10), kind=kOutput, calls=%fused_computation.22 | convolution fusion | flops 2421817344 | bytes 5177344 | tf_op jit(solution)/shard_map/transpose(jvp(lshf,lhe->hsfe))/dot_general | solution.py:49
  519.0 8.5 fusion.61
  528.4 25.0 %fusion = f32[6,1,8,32]{3,1,2,0:T(1,128)S(1)} fusion(f32[2048,6,32]{0,2,1:T(8,128)S(1)} %copy-done.46, f32[2048,8]{0,1:T(8,128)S(1)} %copy-done.33, f32[6,2048,1,1]{1,0,2,3:T(8,128)S(1)} %get-tuple-element.45), kind=kOutput, calls=%fused_computation | convolution fusion | flops 40894464 | bytes 1693696 | tf_op jit(solution)/shard_map/transpose(jvp(lshf,hsf->lh))/dot_general | solution.py:53
  553.3 2.1 fusion.64
  555.5 3.2 convolution_multiply_fusion.1
  558.7 11.9 %multiply_reduce_fusion = f32[6,2048,32]{1,2,0:T(8,128)S(1)} fusion(f32[6,8,32]{2,1,0:T(8,128)S(1)} %bitcast.194, f32[6,2048]{1,0:T(8,128)S(1)} %get-tuple-element.46, f32[2048,8]{0,1:T(8,128)S(1)} %copy-done.33, f32[6,8,32,64]{3,2,1,0:T(8,128)S(1)} %copy-done.49, f32[2048,6,64]{0,2,1:T(8,128)S(1)} %bitcast.182, f32[2048,6]{0,1:T(8,128)S(1)} %bitcast.189), kind=kOutput, calls=%fused_computation.23 | convolution fusion | flops 2428895232 | bytes 5281792 | tf_op jit(solution)/shard_map/transpose(jvp(lshf,hsfe->lhe))/dot_general | solution.py:52
  570.6 4.5 convolution_multiply_fusion
  575.1 1.2 multiply_add_fusion.3
  577.8 2.1 copy-done.9
  579.9 5.8 convolution_convert_fusion
  585.8 1.8 copy-done.41
  587.6 10.6 %fusion.58 = f32[1536,768]{0,1:T(8,128)} fusion(bf16[1,2048,768]{2,1,0:T(8,128)(2,1)S(1)} %copy-done.41, f32[2048,1536]{1,0:T(8,128)} %fusion.104), kind=kOutput, calls=%fused_computation.82 | convolution fusion | flops 4860149760 | bytes 20447232 | tf_op jit(solution)/shard_map/dot_general | solution.py:68
  598.3 1.8 copy-done.40
  600.1 9.8 %fusion.108 = f32[768,1536]{1,0:T(8,128)} fusion(bf16[2048,768]{1,0:T(8,128)(2,1)S(1)} %copy-done.40, bf16[2048,1536]{1,0:T(8,128)(2,1)} %copy-done.47), kind=kOutput, calls=%fused_computation.175 | convolution fusion | flops 4831838208 | bytes 14155776 | tf_op jit(solution)/shard_map/dot_general | solution.py:68
  610.0 1.3 copy-done.13
  611.3 4.9 fusion.107
  616.2 8.6 fusion.52
  624.9 4.4 reduce-scatter.15.cloned.1.call-done
  629.3 2.4 fusion.42
  631.7 2.0 fusion.43
  633.7 39.7 %all-reduce.9 = (f32[768]{0:T(1024)S(1)}, f32[768]{0:T(1024)S(1)}) all-reduce(f32[768]{0:T(1024)S(1)} %get-tuple-element.18, f32[768]{0:T(1024)S(1)} %copy-done.37), channel_id=7, replica_groups=mesh['dp'=16,'mp'=2] {'dp','mp'}, use_global_device_ids=true, to_apply=%region_16.0.clone | all-reduce | flops 1536 | bytes 12288
  674.6 5.3 add_bitcast_fusion
  679.9 30.0 %reduce-scatter.23.cloned.1.call-done = f32[1536,48]{0,1:T(8,128)} async-done(((f32[1536,768]{0,1:T(8,128)}), f32[1536,48]{0,1:T(8,128)}) %reduce-scatter.23.cloned.1.call-update) | async-done | bytes 294928 | tf_op jit(solution)/shard_map/reduce_scatter | solution.py:188
  709.9 79.4 %reduce-scatter.21.cloned.1.call-done = f32[48,1536]{1,0:T(8,128)} async-done(((f32[768,1536]{1,0:T(8,128)}), f32[48,1536]{1,0:T(8,128)}) %reduce-scatter.21.cloned.1.call-update) | async-done | bytes 294928 | tf_op jit(solution)/shard_map/reduce_scatter | solution.py:187
  789.3 61.4 %reduce-scatter.19.cloned.1.call-done = f32[384,48]{0,1:T(8,128)} async-done(((f32[384,768]{0,1:T(8,128)}), f32[384,48]{0,1:T(8,128)}) %reduce-scatter.19.cloned.1.call-update) | async-done | bytes 73744 | tf_op jit(solution)/shard_map/reduce_scatter | solution.py:186
  850.7 71.4 %reduce-scatter.17.cloned.1.call-done = f32[48,3,384]{2,0,1:T(8,128)} async-done(((f32[768,3,384]{2,0,1:T(8,128)}), f32[48,3,384]{2,0,1:T(8,128)}) %reduce-scatter.17.cloned.1.call-update) | async-done | bytes 221200 | tf_op jit(solution)/shard_map/reduce_scatter | solution.py:185
  (140 shorter events, 9.7 us)
Async XLA Ops:
  7.2 236.7 %copy-start = (bf16[768,1536]{1,0:T(8,128)(2,1)S(1)}, bf16[768,1536]{1,0:T(8,128)(2,1)}, u32[]{:S(2)}) copy-start(bf16[768,1536]{1,0:T(8,128)(2,1)} %param.18) | copy-start | bytes 7077892
  7.2 5.1 copy-start.25
  7.2 54.6 %all-gather.6.cloned.1.call-start = ((), (), s32[]{:S(2)}) async-start(), calls=%async_computation.8 | async-start | bytes 4718592 | tf_op jit(solution)/shard_map/all_gather | solution.py:103
  7.2 5.1 copy-start.4
  9.1 2.6 copy-start.22
  11.1 0.6 copy-start.34
  11.7 0.6 copy-start.27
  14.0 3.9 copy-start.38
  14.0 178.7 %reduce-scatter.9.cloned.1.call-start = ((), (), s32[]{:S(2)}) async-start(), calls=%async_computation.9 | async-start | bytes 9437184 | tf_op jit(solution)/shard_map/reduce_scatter | solution.py:107
  18.0 81.8 %copy-start.32 = (f32[2048,8]{0,1:T(8,128)}, f32[2048,8]{0,1:T(8,128)S(1)}, u32[]{:S(2)}) copy-start(f32[2048,8]{0,1:T(8,128)S(1)} %fusion.82) | copy-start | bytes 196612
  19.0 50.0 %copy-start.14 = (f32[2048,32]{0,1:T(8,128)}, f32[2048,32]{0,1:T(8,128)S(1)}, u32[]{:S(2)}) copy-start(f32[2048,32]{0,1:T(8,128)S(1)} %get-tuple-element.48) | copy-start | bytes 786436
  68.2 20.5 %copy-start.10 = (f32[2048,3,6,64]{0,3,2,1:T(8,128)}, f32[2048,3,6,64]{0,3,2,1:T(8,128)S(1)}, u32[]{:S(2)}) copy-start(f32[2048,3,6,64]{0,3,2,1:T(8,128)S(1)} %fusion.50) | copy-start | bytes 28311556
  69.0 1.4 copy-start.24
  73.4 3.2 copy-start.17
  75.7 5.1 copy-start.43
  76.6 12.1 %copy-start.19 = (f32[2048,6,32]{0,2,1:T(8,128)}, f32[2048,6,32]{0,2,1:T(8,128)S(1)}, u32[]{:S(2)}) copy-start(f32[2048,6,32]{0,2,1:T(8,128)S(1)} %add_select_fusion) | copy-start | bytes 4718596
  80.8 19.0 %copy-start.45 = (f32[2048,6,32]{0,2,1:T(8,128)}, f32[2048,6,32]{0,2,1:T(8,128)S(1)}, u32[]{:S(2)}) copy-start(f32[2048,6,32]{0,2,1:T(8,128)S(1)} %get-tuple-element.50) | copy-start | bytes 4718596
  88.6 11.1 %copy-start.30 = (f32[6,1,2048,1]{2,0,1,3:T(8,128)}, f32[6,1,2048,1]{2,0,1,3:T(8,128)S(1)}, u32[]{:S(2)}) copy-start(f32[6,1,2048,1]{2,0,1,3:T(8,128)S(1)} %copy.43) | copy-start | bytes 147460
  99.7 10.1 %copy-start.48 = (f32[6,8,32,64]{3,2,1,0:T(8,128)}, f32[6,8,32,64]{3,2,1,0:T(8,128)S(1)}, u32[]{:S(2)}) copy-start(f32[6,8,32,64]{3,2,1,0:T(8,128)S(1)} %fusion.10) | copy-start | bytes 1179652
  99.8 11.2 %copy-start.21 = (bf16[384,768]{1,0:T(8,128)(2,1)S(1)}, bf16[384,768]{1,0:T(8,128)(2,1)}, u32[]{:S(2)}) copy-start(bf16[384,768]{1,0:T(8,128)(2,1)} %param.16) | copy-start | bytes 1769476
  109.8 1.2 copy-start.12
  115.5 128.3 %all-gather.8.cloned.1.call-start = ((), (), s32[]{:S(2)}) async-start(), calls=%async_computation.10 | async-start | bytes 4718592 | tf_op jit(solution)/shard_map/all_gather | solution.py:110
  195.5 1.7 copy-start.2
  195.5 1.7 copy-start.36
  198.8 91.5 %all-gather.12.cloned.1.call-start = ((), (), s32[]{:S(2)}) async-start(), calls=%async_computation.19 | async-start | bytes 4718592 | tf_op jit(solution)/shard_map/all_gather | solution.py:119
  199.3 193.5 %reduce-scatter.13.cloned.1.call-start = ((), (), s32[]{:S(2)}) async-start(), calls=%async_computation.12 | async-start | bytes 9437184 | tf_op jit(solution)/shard_map/reduce_scatter | solution.py:125
  306.0 2.7 copy-start.47
  315.6 1.7 copy-start.42
  315.6 122.7 %reduce-scatter.11.cloned.1.call-start = ((), (), s32[]{:S(2)}) async-start(), calls=%async_computation.11 | async-start | bytes 4718592 | tf_op jit(solution)/shard_map/reduce_scatter | solution.py:114
  328.9 63.9 %copy-start.3 = (f32[1024,768]{1,0:T(8,128)S(1)}, f32[1024,768]{1,0:T(8,128)}, u32[]{:S(2)}) copy-start(f32[1024,768]{1,0:T(8,128)} %copy-done.2) | copy-start | bytes 9437188
  329.0 162.9 %all-gather.10.cloned.1.call-start = ((), (), s32[]{:S(2)}) async-start(), calls=%async_computation.13 | async-start | bytes 4718592 | tf_op jit(solution)/shard_map/all_gather | solution.py:132
  438.3 4.9 copy-start.7
  443.2 4.1 copy-start.8
  446.8 1.8 copy-start.29
  446.8 182.5 %reduce-scatter.15.cloned.1.call-start = ((), (), s32[]{:S(2)}) async-start(), calls=%async_computation.14 | async-start | bytes 4718592 | tf_op jit(solution)/shard_map/reduce_scatter | solution.py:137
  449.8 45.6 %copy-start.31 = (f32[6,1,2048,1]{2,0,1,3:T(8,128)S(1)}, f32[6,1,2048,1]{2,0,1,3:T(8,128)}, u32[]{:S(2)}) copy-start(f32[6,1,2048,1]{2,0,1,3:T(8,128)} %copy-done.30) | copy-start | bytes 147460
  449.8 45.6 %copy-start.33 = (f32[2048,8]{0,1:T(8,128)S(1)}, f32[2048,8]{0,1:T(8,128)}, u32[]{:S(2)}) copy-start(f32[2048,8]{0,1:T(8,128)} %copy-done.32) | copy-start | bytes 196612
  491.9 3.6 copy-start.46
  506.8 12.2 %copy-start.20 = (f32[2048,6,32]{0,2,1:T(8,128)S(1)}, f32[2048,6,32]{0,2,1:T(8,128)}, u32[]{:S(2)}) copy-start(f32[2048,6,32]{0,2,1:T(8,128)} %copy-done.19) | copy-start | bytes 4718596
  519.0 8.5 copy-start.11
  528.3 25.0 %copy-start.18 = (f32[2048,6,32]{0,2,1:T(8,128)S(1)}, f32[2048,6,32]{0,2,1:T(8,128)}, u32[]{:S(2)}) copy-start(f32[2048,6,32]{0,2,1:T(8,128)} %copy-done.17) | copy-start | bytes 4718596
  528.3 25.0 %copy-start.39 = (s32[1,2048]{1,0:T(1,128)S(1)}, s32[1,2048]{1,0:T(1,128)}, u32[]{:S(2)}) copy-start(s32[1,2048]{1,0:T(1,128)} %param.12) | copy-start | bytes 24580
  555.4 3.2 copy-start.44
  555.5 3.2 copy-start.49
  570.6 4.5 copy-start.15
  577.0 2.9 copy-start.16
  577.8 2.1 copy-start.9
  585.8 1.9 copy-start.41
  585.8 124.1 %reduce-scatter.23.cloned.1.call-start = ((), (), s32[]{:S(2)}) async-start(), calls=%async_computation.18 | async-start | bytes 5013504 | tf_op jit(solution)/shard_map/reduce_scatter | solution.py:188
  598.2 1.9 copy-start.40
  598.2 191.1 %reduce-scatter.21.cloned.1.call-start = ((), (), s32[]{:S(2)}) async-start(), calls=%async_computation.17 | async-start | bytes 5013504 | tf_op jit(solution)/shard_map/reduce_scatter | solution.py:187
  609.9 1.4 copy-start.13
  609.9 240.8 %reduce-scatter.19.cloned.1.call-start = ((), (), s32[]{:S(2)}) async-start(), calls=%async_computation.16 | async-start | bytes 1253376 | tf_op jit(solution)/shard_map/reduce_scatter | solution.py:186
  616.2 305.9 %reduce-scatter.17.cloned.1.call-start = ((), (), s32[]{:S(2)}) async-start(), calls=%async_computation.15 | async-start | bytes 3760128 | tf_op jit(solution)/shard_map/reduce_scatter | solution.py:185
  624.8 4.5 copy-start.5
  624.8 4.5 copy-start.23
  624.8 4.5 copy-start.26
  624.8 6.9 copy-start.35
  624.8 6.9 copy-start.28
  624.8 8.8 copy-start.37
  629.3 2.4 copy-start.6
  674.6 247.5 %copy-start.1 = (bf16[768,1536]{1,0:T(8,128)(2,1)S(1)}, bf16[768,1536]{1,0:T(8,128)(2,1)}, u32[]{:S(2)}) copy-start(bf16[768,1536]{1,0:T(8,128)(2,1)} %param.18) | copy-start | bytes 7077892
Sparse Core Ops, SparseCore 0:
  14.2 47.6 all-gather.5
  115.6 77.0 reduce-scatter.8
  198.9 44.9 all-gather.7
  245.3 44.9 all-gather.11
  315.7 77.0 reduce-scatter.12
  394.9 43.3 reduce-scatter.10
  446.9 44.9 all-gather.9
  585.9 43.3 reduce-scatter.14
  633.7 76.1 reduce-scatter.22
  714.7 74.5 reduce-scatter.20
  793.5 57.1 reduce-scatter.18
  855.0 67.0 reduce-scatter.16
where the time goes:
time: 940 us; the launch traced here: 929 us
  waiting for transfers between devices  595 us (63%)
  matrix products  215 us (23%)
  other arithmetic  41.7 us (4%)
  blocking collectives  39.7 us (4%)
  local copies, waits for them, and re-layouts  20.8 us (2%)
  between operations  15.4 us (2%)
    reduce_scatter x1, waiting for transfers between devices, on_device(): lax.psum_scatter(up_sum, 'dp', scatter_dimension=0, tiled=True)  79.4 us
    reduce_scatter x1, waiting for transfers between devices, heads_pass(): lax.psum_scatter(matmul(attn, out_weight), 'mp', scatter_dimension=0, til...  77.2 us
    reduce_scatter x1, waiting for transfers between devices, on_device(): lax.psum_scatter(qkv_grad, 'dp', scatter_dimension=0, tiled=True)  71.4 us
    reduce_scatter x1, waiting for transfers between devices, heads_pass(): lax.psum_scatter(times_transpose(dhpre, up_weight), 'mp', scatter_dimensi...  63.8 us
    reduce_scatter x1, waiting for transfers between devices, on_device(): lax.psum_scatter(out_grad_w, 'dp', scatter_dimension=1, tiled=True)  61.4 us
    all_gather x1, waiting for transfers between devices, heads_pass(): second_full = lax.all_gather(second, 'mp', axis=0, tiled=True)  44.5 us
    all_gather x1, waiting for transfers between devices, heads_pass(): first_full = lax.all_gather(first, 'mp', axis=0, tiled=True)  42.8 us
    all_gather x1, waiting for transfers between devices, heads_pass(): dbranch_full = lax.all_gather(dbranch, 'mp', axis=0, tiled=True)  42 us
  transfers between devices with their start and end apart: 12, of which 12 were waited for; matrix products, arithmetic and copies ran while one was open for 8% of the time, Pallas kernels for 0%

commit v1 on v0

v1 whole, which is shorter than its diff:
```python
import functools

import jax
import jax.numpy as jnp
from jax import lax
from jax.experimental import pallas as pl
from jax.experimental.pallas import tpu as pltpu
from jax.sharding import PartitionSpec as P

SEGS = 8
BR = 256
PIECES = 16
F32 = jnp.float32
BF16 = jnp.bfloat16
MIB = 1 << 20


def mm(a, b):
    return lax.dot_general(a, b, (((1,), (0,)), ((), ())), preferred_element_type=F32)


def mm_t(a, b):
    return lax.dot_general(a, b, (((1,), (1,)), ((), ())), preferred_element_type=F32)


def norm_parts(v):
    mean = jnp.mean(v, axis=-1, keepdims=True)
    centred = v - mean
    var = jnp.mean(centred * centred, axis=-1, keepdims=True)
    rstd = lax.rsqrt(var + 1e-5)
    return centred * rstd, rstd


def norm_back(da, xhat, rstd, gain):
    dxhat = da * gain
    m1 = jnp.mean(dxhat, axis=-1, keepdims=True)
    m2 = jnp.mean(dxhat * xhat, axis=-1, keepdims=True)
    return rstd * (dxhat - m1 - xhat * m2)


def row_sums(v):
    r, n = v.shape
    return jnp.sum(v.reshape(r // 8, 8, n), axis=0)


def swap_halves(u):
    lane = lax.broadcasted_iota(jnp.int32, u.shape, 1)
    return jnp.where((lane & 63) < 32, pltpu.roll(u, 96, 1), pltpu.roll(u, 32, 1))


def rope(u, cos, sin):
    out = []
    for g in range(u.shape[1] // 128):
        part = u[:, 128 * g : 128 * (g + 1)]
        out.append(part * cos + swap_halves(part) * sin)
    return jnp.concatenate(out, axis=1)


def rope_back(g_, cos, sin):
    out = []
    for g in range(g_.shape[1] // 128):
        part = g_[:, 128 * g : 128 * (g + 1)]
        out.append(part * cos + swap_halves(part * sin))
    return jnp.concatenate(out, axis=1)


def softplus(z):
    return jnp.maximum(z, 0.0) + jnp.log1p(jnp.exp(-jnp.abs(z)))


def head_masks(nf):
    row = lax.broadcasted_iota(jnp.int32, (nf, 128), 0) // 32
    lane = lax.broadcasted_iota(jnp.int32, (nf, 128), 1) // 64
    own = (row & 1) == lane
    masks = [jnp.where(own & (row // 2 == g), 1.0, 0.0).astype(F32) for g in range(nf // 64)]
    other = jnp.where(own, 0.0, 1.0).astype(F32)
    return masks, other


def expand(state, masks):
    turned = pltpu.roll(state, 64, 1)
    parts = [state * m for m in masks] + [turned * m for m in masks]
    return jnp.concatenate(parts, axis=1).astype(BF16)


def fold(wide, masks):
    n = len(masks)
    first = sum(wide[:, 128 * g : 128 * (g + 1)] * m for g, m in enumerate(masks))
    second = sum(wide[:, 128 * (n + g) : 128 * (n + g + 1)] * m for g, m in enumerate(masks))
    return first + pltpu.roll(second, 64, 1)


def store_turned(value, scratch, out_ref, order):
    d = value.shape[1]
    step = d // PIECES
    scratch[...] = jnp.transpose(value).astype(BF16)
    for p in range(PIECES):
        at = pl.multiple_of(order[p] * step, 16)
        out_ref[p * step : (p + 1) * step, :] = scratch[pl.ds(at, step), :]


S_DOC, S_QUARTER, S_LOW = 16, 17, 18


def doc_range(sp, i, nb):
    return sp[S_LOW + i], sp[S_LOW + nb + i] + 1


def assemble_kernel(sp, a, b, c, d, out):
    for k, ref in enumerate((a, b, c, d)):

        @pl.when(pl.program_id(0) == k)
        def _(ref=ref):
            out[...] = ref[...]


def turn_kernel(sp, x, out, scratch):
    store_turned(x[...].astype(F32), scratch, out, sp)


def project(a1, w, cos, sin, om_hi, om_lo, seg_row, sp, pq_o, pk_o, v_o, st_o, i, nb):
    half = w.shape[1] // 3
    nf = om_hi.shape[1]
    c, s = cos[...], sin[...]

    def feature(u):
        turned = rope(u, c, s)
        hi = turned.astype(BF16)
        lo = (turned - hi.astype(F32)).astype(BF16)
        return softplus(mm(hi, om_hi[...]) + mm(lo, om_hi[...]) + mm(hi, om_lo[...]))

    pq_o[...] = feature(mm(a1, w[:, :half]))
    pk = feature(mm(a1, w[:, half : 2 * half]))
    pk_o[...] = pk
    vals = mm(a1, w[:, 2 * half :]).astype(BF16)
    v_o[...] = vals
    masks, other = head_masks(nf)
    pk_t = jnp.transpose(pk)
    right = jnp.concatenate([vals, jnp.ones((vals.shape[0], 128), BF16)], axis=1)

    @pl.when(i == 0)
    def _():
        st_o[...] = jnp.zeros_like(st_o)

    lo_doc, hi_doc = doc_range(sp, i, nb)

    def body(doc, carry):
        left = jnp.where(seg_row[...] == doc, pk_t, 0.0).astype(BF16)
        wide = mm(left, right)
        part = wide[:, half:] * other
        for g, m in enumerate(masks):
            part = part + wide[:, 128 * g : 128 * (g + 1)] * m
        st_o[doc] = st_o[doc] + part
        return carry

    lax.fori_loop(lo_doc, hi_doc, body, 0)


def qkv_first_kernel(
    sp, x, g1, w, cos, sin, om_hi, om_lo, seg_row, a1_o, a1t_o, pq_o, pk_o, v_o, st_o, scratch, *, nb
):
    i = pl.program_id(0)
    xhat, _ = norm_parts(x[...].astype(F32))
    a1f = xhat * g1[...]
    a1 = a1f.astype(BF16)
    a1_o[...] = a1
    store_turned(a1f, scratch, a1t_o, sp)
    project(a1, w, cos, sin, om_hi, om_lo, seg_row, sp, pq_o, pk_o, v_o, st_o, i, nb)


def qkv_second_kernel(
    sp, a1, w, cos, sin, om_hi, om_lo, seg_row, pq_o, pk_o, v_o, st_o, *, nb
):
    i = pl.program_id(0)
    project(a1[...], w, cos, sin, om_hi, om_lo, seg_row, sp, pq_o, pk_o, v_o, st_o, i, nb)


def expand_all(sp, st, other_half, wide, nb):
    masks, _ = head_masks(st.shape[1])

    def body(doc, carry):
        share = jnp.where(doc == sp[S_DOC], 1.0, 0.0)
        wide[doc] = expand(st[doc] + other_half[...] * share, masks)
        return carry

    lax.fori_loop(sp[S_LOW], sp[S_LOW + 2 * nb - 1] + 1, body, 0)


def attend_kernel(
    sp, x, g2, seg_col, pq_l, pq_r, st_l, st_r, ex_l, ex_r, wo_l, wo_r,
    at_l, at_r, x2_o, a2_o, a2t_o, wide_l, wide_r, acc, scratch, *, nb,
):
    i = pl.program_id(0)

    @pl.when(i == 0)
    def _():
        expand_all(sp, st_l, ex_l, wide_l, nb)
        expand_all(sp, st_r, ex_r, wide_r, nb)

    lo_doc, hi_doc = doc_range(sp, i, nb)
    x2 = x[...].astype(F32)
    for pq, wide, wo, at in ((pq_l, wide_l, wo_l, at_l), (pq_r, wide_r, wo_r, at_r)):
        half = wo.shape[0]
        pqb = pq[...].astype(BF16)

        def body(doc, carry, pqb=pqb, wide=wide, half=half):
            nd = mm(pqb, wide[doc])
            acc[...] = jnp.where(seg_col[...] == doc, nd[:, :half] / nd[:, half:], acc[...])
            return carry

        lax.fori_loop(lo_doc, hi_doc, body, 0)
        attn = acc[...].astype(BF16)
        at[...] = attn
        x2 = x2 + mm(attn, wo[...])
    x2_o[...] = x2
    xhat, _ = norm_parts(x2)
    a2f = xhat * g2[...]
    a2_o[...] = a2f.astype(BF16)
    store_turned(a2f, scratch, a2t_o, sp)


GC = 0.7978845608028654


def mlp_kernel(
    a2, a2t, dy, dyt, wu, wd, out_in, da_in,
    out_o, da_o, gu_o, gd_o, hact, dhp, acc_o, acc_d, *, last, has_da,
):
    j = pl.program_id(0)
    nj = pl.num_programs(0)
    rows = a2.shape[0]

    def chunk(r, carry):
        rs = pl.ds(pl.multiple_of(r * BR, BR), BR)
        h = mm(a2[rs, :], wu[...])
        d = mm_t(dy[rs, :], wd[...])
        sq = h * h
        t = jnp.tanh(h * (GC + (GC * 0.044715) * sq))
        half1 = 0.5 + 0.5 * t
        act = (h * half1).astype(BF16)
        slope = half1 + (0.5 * h) * (1.0 - t * t) * (GC + (3 * GC * 0.044715) * sq)
        back = (d * slope).astype(BF16)
        hact[rs, :] = act
        dhp[rs, :] = back
        po = mm(act, wd[...])
        pd = mm_t(back, wu[...])

        @pl.when(j == 0)
        def _():
            acc_o[rs, :] = out_in[rs, :] + po
            if has_da:
                acc_d[rs, :] = da_in[rs, :] + pd
            else:
                acc_d[rs, :] = pd

        @pl.when(j > 0)
        def _():
            acc_o[rs, :] = acc_o[rs, :] + po
            acc_d[rs, :] = acc_d[rs, :] + pd

        @pl.when(j == nj - 1)
        def _():
            out_o[rs, :] = acc_o[rs, :].astype(out_o.dtype)
            da_o[rs, :] = acc_d[rs, :]

        return carry

    lax.fori_loop(0, rows // BR, chunk, 0)

    def grads(r, carry):
        rs = pl.ds(pl.multiple_of(r * BR, BR), BR)
        gu_o[rs, :] = mm(a2t[rs, :], dhp[...]).astype(BF16)
        gd_o[rs, :] = mm(dyt[rs, :], hact[...]).astype(BF16)
        return carry

    lax.fori_loop(0, a2t.shape[0] // BR, grads, 0)


def back_one_kernel(
    sp, x2, da2, dy, g2, seg_col, seg_row, cos, sin, om, pq_l, pq_r, st_l, st_r, ex_l, ex_r, wo_l, wo_r,
    dx2_o, dbt_o, gain_o, dq_l, dq_r, dst_l, dst_r, wide_l, wide_r, attn_s, inv_s, dpq_s, scratch, *, nb,
):
    i = pl.program_id(0)

    @pl.when(i == 0)
    def _():
        expand_all(sp, st_l, ex_l, wide_l, nb)
        expand_all(sp, st_r, ex_r, wide_r, nb)
        gain_o[...] = jnp.zeros_like(gain_o)
        dst_l[...] = jnp.zeros_like(dst_l)
        dst_r[...] = jnp.zeros_like(dst_r)

    xhat, rstd = norm_parts(x2[...])
    da = da2[...]
    gain_o[...] += row_sums(da * xhat)
    dx2 = dy[...].astype(F32) + norm_back(da, xhat, rstd, g2[...])
    dx2_o[...] = dx2
    datt = dx2.astype(BF16)
    store_turned(dx2, scratch, dbt_o, sp)
    lo_doc, hi_doc = doc_range(sp, i, nb)
    for pq, wide, wo, dq, dst in (
        (pq_l, wide_l, wo_l, dq_l, dst_l),
        (pq_r, wide_r, wo_r, dq_r, dst_r),
    ):
        half = wo.shape[0]
        masks, _ = head_masks(pq.shape[1])
        pqf = pq[...]
        pqb = pqf.astype(BF16)

        def first(doc, carry, pqb=pqb, wide=wide, half=half):
            nd = mm(pqb, wide[doc])
            here = seg_col[...] == doc
            inv = 1.0 / nd[:, half:]
            attn_s[...] = jnp.where(here, nd[:, :half] * inv, attn_s[...])
            inv_s[...] = jnp.where(here, inv, inv_s[...])
            return carry

        lax.fori_loop(lo_doc, hi_doc, first, 0)
        dnum = mm_t(datt, wo[...]) * inv_s[...]
        both = jnp.concatenate([dnum, -dnum * attn_s[...]], axis=1).astype(BF16)
        pq_t = jnp.transpose(pqf)

        def second(doc, carry, both=both, pq_t=pq_t, wide=wide, dst=dst, masks=masks):
            dpq_s[...] = jnp.where(seg_col[...] == doc, mm_t(both, wide[doc]), dpq_s[...])
            left = jnp.where(seg_row[...] == doc, pq_t, 0.0).astype(BF16)
            dst[doc] = dst[doc] + fold(mm(left, both), masks)
            return carry

        lax.fori_loop(lo_doc, hi_doc, second, 0)
        dz = (dpq_s[...] * (1.0 - jnp.exp(-pqf))).astype(BF16)
        dq[...] = rope_back(mm_t(dz, om[...]), cos[...], sin[...]).astype(BF16)


def back_two_kernel(
    sp, seg_col, cos, sin, om, pk_l, pk_r, v_l, v_r, dst_l, dst_r, ex_l, ex_r,
    dk_l, dv_l, dk_r, dv_r, wide_l, wide_r, dpk_s, dv_s, *, nb,
):
    i = pl.program_id(0)

    @pl.when(i == 0)
    def _():
        expand_all(sp, dst_l, ex_l, wide_l, nb)
        expand_all(sp, dst_r, ex_r, wide_r, nb)

    lo_doc, hi_doc = doc_range(sp, i, nb)
    for pk, v, wide, dk, dv in (
        (pk_l, v_l, wide_l, dk_l, dv_l),
        (pk_r, v_r, wide_r, dk_r, dv_r),
    ):
        half = v.shape[1]
        pkf = pk[...]
        pkb = pkf.astype(BF16)
        right = jnp.concatenate([v[...], jnp.ones(v.shape, BF16)], axis=1)

        def body(doc, carry, pkb=pkb, right=right, wide=wide, half=half):
            here = seg_col[...] == doc
            dpk_s[...] = jnp.where(here, mm_t(right, wide[doc]), dpk_s[...])
            dv_s[...] = jnp.where(here, mm(pkb, wide[doc, :, :half]), dv_s[...])
            return carry

        lax.fori_loop(lo_doc, hi_doc, body, 0)
        dv[...] = dv_s[...].astype(BF16)
        dz = (dpk_s[...] * (1.0 - jnp.exp(-pkf))).astype(BF16)
        dk[...] = rope_back(mm_t(dz, om[...]), cos[...], sin[...]).astype(BF16)


def input_kernel(x, g1, dx2, dq_l, dk_l, dv_l, dq_r, dk_r, dv_r, w_l, w_r, dx_o, gain_o):
    i = pl.program_id(0)
    half = w_l.shape[1] // 3

    @pl.when(i == 0)
    def _():
        gain_o[...] = jnp.zeros_like(gain_o)

    da = None
    for w, parts in ((w_l, (dq_l, dk_l, dv_l)), (w_r, (dq_r, dk_r, dv_r))):
        for k, part in enumerate(parts):
            term = mm_t(part[...], w[:, half * k : half * (k + 1)])
            da = term if da is None else da + term
    xhat, rstd = norm_parts(x[...].astype(F32))
    gain_o[...] += row_sums(da * xhat)
    dx_o[...] = dx2[...] + norm_back(da, xhat, rstd, g1[...])


def whole(shape):
    zeros = (0,) * len(shape)
    return pl.BlockSpec(tuple(shape), lambda i, *_: zeros)


def by_rows(shape, br=BR):
    return pl.BlockSpec((br, shape[1]), lambda i, *_: (i, 0))


def by_cols(shape, bc=BR):
    return pl.BlockSpec((shape[0], bc), lambda i, *_: (0, i))


def call(kernel, grid, scalars, ins, outs, scratch, flops, vmem=56):
    args = [a for a, _ in ins]
    moved = sum(a.size * a.dtype.itemsize for a in args)
    for shape, dtype, _ in outs:
        size = 1
        for n in shape:
            size *= n
        moved += size * jnp.dtype(dtype).itemsize
    prefetch = [] if scalars is None else [scalars]
    return pl.pallas_call(
        kernel,
        out_shape=[jax.ShapeDtypeStruct(s, d) for s, d, _ in outs],
        grid_spec=pltpu.PrefetchScalarGridSpec(
            num_scalar_prefetch=len(prefetch),
            grid=grid,
            in_specs=[s for _, s in ins],
            out_specs=[s for _, _, s in outs],
            scratch_shapes=scratch,
        ),
        compiler_params=pltpu.CompilerParams(
            dimension_semantics=("arbitrary",) * len(grid), vmem_limit_bytes=vmem * MIB
        ),
        cost_estimate=pl.CostEstimate(flops=flops, bytes_accessed=moved, transcendentals=0),
    )(*prefetch, *args)


class Links:
    def __init__(self, n_dp, n_mp):
        self.n_dp, self.n_mp = n_dp, n_mp
        self.fine = n_dp // PIECES

    def dp_xor(self, v, bits):
        pairs = [(d, d ^ bits) for d in range(self.n_dp)]
        return lax.ppermute(v, "dp", pairs)

    def mp_swap(self, v):
        return lax.ppermute(v, "mp", [(m, m ^ 1) for m in range(self.n_mp)])


def add(a, b):
    return (a.astype(F32) + b.astype(F32)).astype(BF16)


def gather_other(links, w, quarter):
    n = w.shape[0] // 4
    own = lax.dynamic_slice_in_dim(w, quarter * n, n, 0)
    first = links.mp_swap(own)
    second = links.dp_xor(first, 2)
    third = links.dp_xor(first, 1)
    fourth = links.dp_xor(second, 1)
    return first, third, second, fourth


def assemble(pieces, scalars):
    n, cols = pieces[0].shape
    out = pl.BlockSpec((n, cols), lambda i, sp: (sp[S_QUARTER] ^ i, 0))
    return call(
        assemble_kernel, (4,), scalars, [(p, whole(p.shape)) for p in pieces],
        [((4 * n, cols), BF16, out)], [], 0,
    )[0]


def finish(links, part):
    fine = links.fine
    step = part.shape[0] // 4
    total = part[:step].astype(F32)
    for r, bits in ((1, 8), (2, 4), (3, 12)):
        total = total + links.dp_xor(part[r * step : (r + 1) * step], bits * fine).astype(F32)
    bit = fine // 2
    me = lax.axis_index("dp")
    while bit:
        half = total.shape[0] // 2
        upper = (me // bit) % 2
        send = lax.dynamic_slice_in_dim(total, (1 - upper) * half, half, 0)
        keep = lax.dynamic_slice_in_dim(total, upper * half, half, 0)
        total = keep + links.dp_xor(send, bit)
        bit //= 2
    return total


def reduce_core(links, g):
    half = g.shape[0] // 2
    return add(g[:half], links.dp_xor(g[half:], links.fine))


def reduce_x(links, g):
    half = g.shape[0] // 2
    return add(g[:half], links.dp_xor(g[half:], 2 * links.fine))


def reduce_rows_first(links, mine, other):
    mine, other = reduce_core(links, mine), reduce_core(links, other)
    both = add(mine, links.mp_swap(other))
    return finish(links, reduce_x(links, both))


def reduce_cols_first(links, mine, other):
    mine, other = reduce_core(links, mine), reduce_core(links, other)
    mine, other = reduce_x(links, mine), reduce_x(links, other)
    return finish(links, add(mine, links.mp_swap(other)))


def sum_everywhere(links, v):
    bit = 1
    while bit < links.n_dp:
        v = v + links.dp_xor(v, bit)
        bit *= 2
    return v + links.mp_swap(v)


def rotary_tables(first, rows, head_size):
    places = first + jnp.arange(rows)
    rates = 10000.0 ** (-(jnp.arange(head_size // 2).astype(F32) * 2.0 / head_size))
    angles = places.astype(F32)[:, None] * rates[None, :]
    cos, sin = jnp.cos(angles), jnp.sin(angles)
    return jnp.concatenate([cos] * 4, 1), jnp.concatenate([-sin, sin, -sin, sin], 1)


def block_omega(omega, heads):
    hd, feat = omega.shape
    scaled = omega * hd ** (-0.25)
    eye = jnp.eye(heads, dtype=F32)
    wide = (eye[:, None, :, None] * scaled[None, :, None, :]).reshape(heads * hd, heads * feat)
    hi = wide.astype(BF16)
    lo = (wide - hi.astype(F32)).astype(BF16)
    return hi, lo


def on_device(
    n_dp, n_mp, inputs, seg_ids, omega, norm1_gain, qkv_weight, out_weight, norm2_gain, up_weight, down_weight, out_grad
):
    links = Links(n_dp, n_mp)
    x, dy = inputs[0], out_grad[0]
    rows, width = x.shape
    nb = rows // BR
    dp, mp = lax.axis_index("dp"), lax.axis_index("mp")
    quarter = dp % 4
    half = out_weight.shape[0]
    heads = half // omega.shape[0]
    nf = heads * omega.shape[1]
    ff = up_weight.shape[1]

    wq_mine = qkv_weight.reshape(width, -1)
    wq_pieces = gather_other(links, wq_mine, quarter)
    wo_pieces = gather_other(links, out_weight, quarter)
    wu_pieces = gather_other(links, up_weight, quarter)
    wd_pieces = gather_other(links, down_weight, quarter)

    seg_all = seg_ids[0]
    seg = lax.dynamic_slice_in_dim(seg_all, mp * rows, rows, 0)
    shared = jnp.where(seg_all[rows - 1] == seg_all[rows], seg_all[rows], -1)
    coarse = dp // links.fine
    order = [int(format(p, "04b")[::-1], 2) for p in range(PIECES)]
    by_block = seg.reshape(nb, BR)
    scalars = jnp.concatenate(
        [jnp.array(order, jnp.int32) ^ coarse, jnp.stack([shared, quarter]), by_block[:, 0], by_block[:, -1]]
    ).astype(jnp.int32)
    seg_col, seg_row = seg.reshape(rows, 1), seg.reshape(1, rows)
    cos, sin = rotary_tables(mp * rows, rows, omega.shape[0])
    om_hi, om_lo = block_omega(omega, heads)
    g1, g2 = norm1_gain.reshape(1, -1), norm2_gain.reshape(1, -1)
    turn_scratch = pltpu.VMEM((width, BR), BF16)
    turned_out = ((width, rows), BF16, by_cols((width, rows)))

    def rowed(n, dtype):
        return ((rows, n), dtype, by_rows((rows, n)))

    def ws(a):
        return (a, whole(a.shape))

    def rs(a):
        return (a, by_rows(a.shape))

    def cs(a):
        return (a, by_cols(a.shape))

    state_out = ((SEGS, nf, 128), F32, whole((SEGS, nf, 128)))
    side = [rs(cos), rs(sin), ws(om_hi), ws(om_lo), cs(seg_row)]
    one_flops = 2 * rows * width * 3 * half
    a1, a1t, pq_l, pk_l, v_l, st_l = call(
        functools.partial(qkv_first_kernel, nb=nb), (nb,), scalars,
        [rs(x), ws(g1), ws(wq_mine)] + side,
        [rowed(width, BF16), turned_out, rowed(nf, F32), rowed(nf, F32), rowed(half, BF16), state_out],
        [turn_scratch], one_flops,
    )
    dyt = call(turn_kernel, (nb,), scalars, [rs(dy)], [turned_out], [turn_scratch], 0)[0]

    def exchange(state):
        return links.mp_swap(lax.dynamic_index_in_dim(state, seg_all[rows - 1], 0, keepdims=False))

    ex_r = exchange(st_l)
    wq_other = assemble(wq_pieces, scalars)
    pq_r, pk_r, v_r, st_r = call(
        functools.partial(qkv_second_kernel, nb=nb), (nb,), scalars,
        [rs(a1), ws(wq_other)] + side,
        [rowed(nf, F32), rowed(nf, F32), rowed(half, BF16), state_out],
        [], one_flops,
    )
    ex_l = exchange(st_r)
    wo_other = assemble(wo_pieces, scalars)
    wide_scratch = pltpu.VMEM((SEGS, nf, 2 * half), BF16)
    at_l, at_r, x2, a2, a2t = call(
        functools.partial(attend_kernel, nb=nb), (nb,), scalars,
        [rs(x), ws(g2), rs(seg_col), rs(pq_l), rs(pq_r), ws(st_l), ws(st_r), ws(ex_l), ws(ex_r),
         ws(out_weight), ws(wo_other)],
        [rowed(half, BF16), rowed(half, BF16), rowed(width, F32), rowed(width, BF16), turned_out],
        [wide_scratch, wide_scratch, pltpu.VMEM((BR, half), F32), turn_scratch],
        2 * rows * width * 2 * half,
    )

    bf = 512
    wu_other = assemble(wu_pieces, scalars)
    wd_other = assemble(wd_pieces, scalars)

    def mlp(wu, wd, out_in, da_in, last):
        has_da = da_in is not None
        da_arg = [ws(da_in)] if has_da else []
        kernel = functools.partial(mlp_kernel, last=last, has_da=has_da)
        if not has_da:

            def kernel(a2_, a2t_, dy_, dyt_, wu_, wd_, oi_, *rest):
                return mlp_kernel(a2_, a2t_, dy_, dyt_, wu_, wd_, oi_, None, *rest, last=last, has_da=False)

        return call(
            kernel, (ff // bf,), None,
            [ws(a2), ws(a2t), ws(dy), ws(dyt), (wu, by_cols(wu.shape, bf)), (wd, by_rows(wd.shape, bf)), ws(out_in)]
            + da_arg,
            [((rows, width), BF16 if last else F32, whole((rows, width))), ((rows, width), F32, whole((rows, width))),
             ((width, ff), BF16, by_cols((width, ff), bf)), ((width, ff), BF16, by_cols((width, ff), bf))],
            [pltpu.VMEM((rows, bf), BF16), pltpu.VMEM((rows, bf), BF16),
             pltpu.VMEM((rows, width), F32), pltpu.VMEM((rows, width), F32)],
            6 * 2 * rows * width * ff,
        )

    part_out, part_da, gu_r, gd_r = mlp(wu_other, wd_other, x2, None, False)
    output, da2, gu_l, gd_l = mlp(up_weight, down_weight, part_out, part_da, True)
    down_sum = jnp.transpose(reduce_rows_first(links, gd_l, gd_r))
    up_sum = reduce_cols_first(links, gu_l, gu_r)

    gain8 = ((8, width), F32, whole((8, width)))
    dx2, dbt, gain2, dq_l, dq_r, dst_l, dst_r = call(
        functools.partial(back_one_kernel, nb=nb), (nb,), scalars,
        [rs(x2), rs(da2), rs(dy), ws(g2), rs(seg_col), cs(seg_row), rs(cos), rs(sin), ws(om_hi),
         rs(pq_l), rs(pq_r), ws(st_l), ws(st_r), ws(ex_l), ws(ex_r), ws(out_weight), ws(wo_other)],
        [rowed(width, F32), turned_out, gain8, rowed(half, BF16), rowed(half, BF16), state_out, state_out],
        [wide_scratch, wide_scratch, pltpu.VMEM((BR, half), F32), pltpu.VMEM((BR, half), F32),
         pltpu.VMEM((BR, nf), F32), turn_scratch],
        2 * rows * width * 2 * half,
    )
    dex_r, dex_l = exchange(dst_l), exchange(dst_r)

    def outer(left, right):
        return lax.dot_general(left, right, (((1,), (0,)), ((), ())), preferred_element_type=F32).astype(BF16)

    out_sum = jnp.transpose(reduce_rows_first(links, outer(dbt, at_l), outer(dbt, at_r)))
    gq_l, gq_r = outer(a1t, dq_l), outer(a1t, dq_r)
    q_sum = reduce_cols_first(links, gq_l, gq_r)
    dk_l, dv_l, dk_r, dv_r = call(
        functools.partial(back_two_kernel, nb=nb), (nb,), scalars,
        [rs(seg_col), rs(cos), rs(sin), ws(om_hi), rs(pk_l), rs(pk_r), rs(v_l), rs(v_r),
         ws(dst_l), ws(dst_r), ws(dex_l), ws(dex_r)],
        [rowed(half, BF16)] * 4,
        [wide_scratch, wide_scratch, pltpu.VMEM((BR, nf), F32), pltpu.VMEM((BR, half), F32)],
        2 * rows * width * half,
    )
    k_sum = reduce_cols_first(links, outer(a1t, dk_l), outer(a1t, dk_r))
    v_sum = reduce_rows_first(links, outer(a1t, dv_l), outer(a1t, dv_r))
    input_grad, gain1 = call(
        input_kernel, (nb,), None,
        [rs(x), ws(g1), rs(dx2), rs(dq_l), rs(dk_l), rs(dv_l), rs(dq_r), rs(dk_r), rs(dv_r), ws(wq_mine), ws(wq_other)],
        [rowed(width, F32), gain8], [], 2 * one_flops,
    )
    gains = sum_everywhere(links, jnp.stack([gain1.sum(0), gain2.sum(0)]))
    share = width // (n_dp * n_mp)
    gains = lax.dynamic_slice_in_dim(gains, (dp * n_mp + mp) * share, share, 1)
    qkv_sum = jnp.stack([q_sum, k_sum, v_sum], axis=1)
    return (output[None], input_grad[None], gains[0], qkv_sum, out_sum, gains[1], up_sum, down_sum)


def solution(mesh):
    n_dp, n_mp = mesh.shape["dp"], mesh.shape["mp"]
    return jax.shard_map(
        functools.partial(on_device, n_dp, n_mp),
        mesh=mesh,
        in_specs=(
            P("dp", "mp", None),
            P("dp", None),
            P(),
            P(),
            P(None, None, "mp"),
            P("mp", None),
            P(),
            P(None, "mp"),
            P("mp", None),
            P("dp", "mp", None),
        ),
        out_specs=(
            P("dp", "mp", None),
            P("dp", "mp", None),
            P(("dp", "mp")),
            P("dp", None, "mp"),
            P("mp", "dp"),
            P(("dp", "mp")),
            P("dp", "mp"),
            P("mp", "dp"),
        ),
        check_vma=False,
    )
```

time: 940 us -> 428 us (0.46); the launches traced: 929 us -> 428 us
  waiting for transfers between devices: 595 us -> 108 us
  matrix products: 215 us -> 12.5 us
  Pallas kernels: 0 us -> 164 us
  starting transfers between devices: 0.96 us -> 86.7 us
  blocking collectives: 39.7 us -> 0 us
  other arithmetic: 41.7 us -> 14.3 us
  local copies, waits for them, and re-layouts: 20.8 us -> 35.9 us
  between operations: 15.4 us -> 5.43 us
    reduce_scatter x8 -> x0, waiting for transfers between devices: 429 us -> none  [the longest x1 79.4 us: on_device(): lax.psum_scatter(up_sum, 'dp', scatter_dimension=0, tiled=True)]
    dot_general x26 -> x8, matrix products: 215 us -> 12.5 us  [outer(): lax.dot_general(left, right, (((1,), (0,)), ((), ())), preferred_element_...]
    all_gather x4 -> x0, waiting for transfers between devices: 166 us -> none  [the longest x1 44.5 us: heads_pass(): second_full = lax.all_gather(second, 'mp', axis=0, tiled=True)]
    pallas_call x0 -> x13, Pallas kernels: none -> 164 us  [call(): pl.pallas_call(kernel, out_shape=[jax.ShapeDtypeStruct(s, d) for s, d, _...]
    ppermute x0 -> x70, waiting for transfers between devices: none -> 108 us  [the longest x55 61.7 us: dp_xor(): return lax.ppermute(v, 'dp', pairs)]
    ppermute x0 -> x70, starting transfers between devices: none -> 86.7 us  [the longest x55 53.9 us: dp_xor(): return lax.ppermute(v, 'dp', pairs)]
    unnamed x1 -> x0, blocking collectives: 39.7 us -> none
    reduce_sum x9 -> x2, other arithmetic: 20.5 us -> 1.5 us  [on_device(): gains = sum_everywhere(links, jnp.stack([gain1.sum(0), gain2.sum(0)]))]
  transfers between devices with their start and end apart: 12 -> 70, of which waited for: 12 -> 35; matrix products, arithmetic and copies ran while one was open for 8% -> 11% of each run, Pallas kernels for 0% -> 31%
where the time goes in v1:
time: 428 us
  Pallas kernels  164 us (38%)
  waiting for transfers between devices  108 us (25%)
  starting transfers between devices  86.7 us (20%)
  local copies, waits for them, and re-layouts  35.9 us (8%)
  other arithmetic  14.3 us (3%)
  matrix products  12.5 us (3%)
  between operations  5.43 us (1%)
    pallas_call x13, Pallas kernels, call(): pl.pallas_call(kernel, out_shape=[jax.ShapeDtypeStruct(s, d) for s, d, _...  164 us
    ppermute x55, waiting for transfers between devices, dp_xor(): return lax.ppermute(v, 'dp', pairs)  61.7 us
    ppermute x55, starting transfers between devices, dp_xor(): return lax.ppermute(v, 'dp', pairs)  53.9 us
    ppermute x15, waiting for transfers between devices, mp_swap(): return lax.ppermute(v, 'mp', [(m, m ^ 1) for m in range(self.n_mp)])  46.7 us
    ppermute x15, starting transfers between devices, mp_swap(): return lax.ppermute(v, 'mp', [(m, m ^ 1) for m in range(self.n_mp)])  32.8 us
    dot_general x8, matrix products, outer(): lax.dot_general(left, right, (((1,), (0,)), ((), ())), preferred_element_...  12.5 us
    unnamed x83, local copies, waits for them, and re-layouts  9.12 us
  transfers between devices with their start and end apart: 70, of which 35 were waited for; matrix products, arithmetic and copies ran while one was open for 11% of the time, Pallas kernels for 31%

profile of v1, /device:TPU:0, one launch (start us, length us, event | category | flops | bytes accessed | tf_op | source)
XLA Modules:
  0.0 427.5 jit_solution(16273937279590754044)
XLA Ops:
  0.7 2.6 copy.39
  5.2 3.0 collective-permute-start
  8.2 1.9 constant_dynamic-slice_fusion.3
  10.1 1.9 constant_dynamic-slice_fusion.2
  12.0 2.0 collective-permute-start.14
  17.3 1.9 fusion
  19.5 2.0 collective-permute-start.2
  25.3 1.9 pad_maximum_fusion
  27.2 4.9 %collective-permute-done.10.a = bf16[192,1536]{1,0:T(8,128)(2,1)} collective-permute-done((bf16[192,1536]{1,0:T(8,128)(2,1)}, bf16[192,1536]{1,0:T(8,128)(2,1)}, u32[]{:S(2)}, u32[]{:S(2)}) %collective-permute-start.10) | collective-permute-done | bytes 589856 | tf_op jit(solution)/shard_map/ppermute | solution.py:434
  32.1 2.0 collective-permute-start.12
  34.2 9.8 %collective-permute-done.14.a = bf16[384,768]{1,0:T(8,128)(2,1)} collective-permute-done((bf16[384,768]{1,0:T(8,128)(2,1)}, bf16[384,768]{1,0:T(8,128)(2,1)}, u32[]{:S(2)}, u32[]{:S(2)}) %collective-permute-start.14) | collective-permute-done | bytes 589856 | tf_op jit(solution)/shard_map/ppermute | solution.py:434
  45.6 12.6 %shard_map.170 = (bf16[1024,768]{1,0:T(8,128)(2,1)}, bf16[768,1024]{1,0:T(8,128)(2,1)}, f32[1024,192]{1,0:T(8,128)}, f32[1024,192]{1,0:T(8,128)}, bf16[1024,384]{1,0:T(8,128)(2,1)}, /*index=5*/f32[8,192,128]{2,1,0:T(8,128)}) custom-call(s32[26]{0:T(128)} %concatenate.9.sp, bf16[1024,768]{1,0:T(8,128)(2,1)} %bitcast.55, f32[1,768]{1,0:T(1,128)} %reshape.68.g1, ...), custom_call_target="tpu_custom_call" | custom-call | flops 1811939328 | bytes 10984448 | tf_op jit(solution)/shard_map/pallas_call | solution.py:407
  61.1 2.2 collective-permute-start.5
  65.9 2.0 collective-permute-start.6
  67.9 3.1 collective-permute-done.6.a
  71.6 4.6 %collective-permute-done.8.c = bf16[96,768]{1,0:T(8,128)(2,1)S(1)} collective-permute-done((bf16[96,768]{1,0:T(8,128)(2,1)S(1)}, bf16[96,768]{1,0:T(8,128)(2,1)S(1)}, u32[]{:S(2)}, u32[]{:S(2)}) %collective-permute-start.8) | collective-permute-done | bytes 147488 | tf_op jit(solution)/shard_map/ppermute | solution.py:431
  78.1 3.9 shard_map.171.w.w_r
  82.3 11.4 %shard_map.172 = (f32[1024,192]{1,0:T(8,128)}, f32[1024,192]{1,0:T(8,128)}, bf16[1024,384]{1,0:T(8,128)(2,1)}, f32[8,192,128]{2,1,0:T(8,128)}) custom-call(s32[26]{0:T(128)} %concatenate.9.sp, bf16[1024,768]{1,0:T(8,128)(2,1)} %get-tuple-element.45.a1, bf16[768,1152]{1,0:T(8,128)(2,1)} %shard_map.171.w.w_r, f32[1024,128]{1,0:T(8,128)} %get-tuple-element.111.cos, ...), custom_call_target="tpu_custom_call" | custom-call | flops 1811939328 | bytes 7835648 | tf_op jit(solution)/shard_map/pallas_call | solution.py:407
  95.9 2.7 collective-permute-start.4
  100.2 4.7 %shard_map.175.dyt_.dyt = bf16[768,1024]{1,0:T(8,128)(2,1)} custom-call(s32[26]{0:T(128)} %concatenate.9.sp, bf16[1024,768]{1,0:T(8,128)(2,1)} %bitcast.51), custom_call_target="tpu_custom_call" | custom-call | bytes 3145728 | tf_op jit(solution)/shard_map/pallas_call | solution.py:407
  104.9 3.3 shard_map.173.wo_r
  108.1 12.5 %shard_map.174 = (bf16[1024,384]{1,0:T(8,128)(2,1)}, bf16[1024,384]{1,0:T(8,128)(2,1)}, f32[1024,768]{1,0:T(8,128)}, bf16[1024,768]{1,0:T(8,128)(2,1)}, bf16[768,1024]{1,0:T(8,128)(2,1)}) custom-call(s32[26]{0:T(128)} %concatenate.9.sp, bf16[1024,768]{1,0:T(8,128)(2,1)} %bitcast.56, f32[1,768]{1,0:T(1,128)} %reshape.66.g2, s32[1024,1]{1,0:T(8,128)} %copy.45.seg_col, ...), custom_call_target="tpu_custom_call" | custom-call | flops 1207959552 | bytes 13966336 | tf_op jit(solution)/shard_map/pallas_call | solution.py:407
  122.2 4.3 shard_map.176.wu_
  128.1 4.2 shard_map.177.wd_
  132.4 29.5 %shard_map.178 = (f32[1024,768]{1,0:T(8,128)}, f32[1024,768]{1,0:T(8,128)}, bf16[768,1536]{1,0:T(8,128)(2,1)}, bf16[768,1536]{1,0:T(8,128)(2,1)}) custom-call(bf16[1024,768]{1,0:T(8,128)(2,1)} %get-tuple-element.49.a2_.a2, bf16[768,1024]{1,0:T(8,128)(2,1)} %get-tuple-element.50.a2t_.a2t, bf16[1024,768]{1,0:T(8,128)(2,1)} %bitcast.52, ...), custom_call_target="tpu_custom_call" | custom-call | flops 14495514624 | bytes 25165824 | tf_op jit(solution)/shard_map/pallas_call | solution.py:407
  161.9 2.4 slice.288
  164.3 29.9 %shard_map.179 = (bf16[1024,768]{1,0:T(8,128)(2,1)}, f32[1024,768]{1,0:T(8,128)}, bf16[768,1536]{1,0:T(8,128)(2,1)}, bf16[768,1536]{1,0:T(8,128)(2,1)}) custom-call(bf16[1024,768]{1,0:T(8,128)(2,1)} %get-tuple-element.49.a2_.a2, bf16[768,1024]{1,0:T(8,128)(2,1)} %get-tuple-element.50.a2t_.a2t, bf16[1024,768]{1,0:T(8,128)(2,1)} %bitcast.53, ...), custom_call_target="tpu_custom_call" | custom-call | flops 14495514624 | bytes 26738688 | tf_op jit(solution)/shard_map/pallas_call | solution.py:407
  194.1 2.5 slice.286
  200.3 24.5 %shard_map.180 = (f32[1024,768]{1,0:T(8,128)}, bf16[768,1024]{1,0:T(8,128)(2,1)}, f32[8,768]{1,0:T(8,128)}, bf16[1024,384]{1,0:T(8,128)(2,1)}, bf16[1024,384]{1,...) custom-call(s32[26]{0:T(128)} %concatenate.9.sp, f32[1024,768]{1,0:T(8,128)} %get-tuple-element.51.oi_.x2, ...), custom_call_target="tpu_custom_call" | custom-call | flops 1207959552 | bytes 21482496 | tf_op jit(solution)/shard_map/pallas_call | solution.py:407
  224.8 3.0 convolution_convert_fusion.7
  227.9 1.8 convolution_convert_fusion.6
  231.2 7.2 %collective-permute-start.19 = (f32[192,128]{1,0:T(8,128)}, f32[192,128]{1,0:T(8,128)}, u32[]{:S(2)}, u32[]{:S(2)}) collective-permute-start(f32[192,128]{1,0:T(8,128)} %dynamic-slice_bitcast_fusion), channel_id=1, source_target_pairs={{0,1},{1,0},{2,3},{3,2},{4,5},{5,4},{6,7},{7,6},{8,9},{9,8},{10,11... | collective-permute-start | bytes 294920 | tf_op jit(solution)/shard_map/ppermute | solution.py:434
  245.0 12.5 %shard_map.181 = (bf16[1024,384]{1,0:T(8,128)(2,1)}, bf16[1024,384]{1,0:T(8,128)(2,1)}, bf16[1024,384]{1,0:T(8,128)(2,1)}, bf16[1024,384]{1,0:T(8,128)(2,1)}) custom-call(s32[26]{0:T(128)} %concatenate.9.sp, s32[1024,1]{1,0:T(8,128)} %copy.45.seg_col, f32[1024,128]{1,0:T(8,128)} %get-tuple-element.111.cos, f32[1024,128]{1,0:T(8,128)} %get-tuple-element.112.sin, ...), custom_call_target="tpu_custom_call" | custom-call | flops 603979776 | bytes 9261056 | tf_op jit(solution)/shard_map/pallas_call | solution.py:407
  257.5 11.1 %shard_map.182 = (f32[1024,768]{1,0:T(8,128)}, f32[8,768]{1,0:T(8,128)}) custom-call(bf16[1024,768]{1,0:T(8,128)(2,1)} %bitcast.57, f32[1,768]{1,0:T(1,128)} %reshape.68.g1, f32[1024,768]{1,0:T(8,128)} %get-tuple-element.56.dx2, bf16[1024,384]{1,0:T(8,128)(2,1)} %get-tuple-element.57.dq_l, bf16[1024,384]{1,0:T(8,128)(2,1)} %get-tuple-element.64.dk_l, ...), custom_call_target="tpu_custom_call" | custom-call | flops 3623878656 | bytes 16149504 | tf_op jit(solution)/shard_map/pallas_call | solution.py:407
  269.4 2.7 convolution_convert_fusion
  274.3 2.3 collective-permute-done.21
  276.6 3.5 collective-permute-start.22
  281.7 2.6 collective-permute-start.23
  286.3 5.1 %collective-permute-start.24 = (f32[2,768]{1,0:T(2,128)S(1)}, f32[2,768]{1,0:T(2,128)S(1)}, u32[]{:S(2)}, u32[]{:S(2)}) collective-permute-start(f32[2,768]{1,0:T(2,128)S(1)} %add.202), channel_id=1, source_target_pairs={{0,1},{1,0},{2,3},{3,2},{4,5},{5,4},{6,7},{7,6},{8,9},{9,8},{10,11... | collective-permute-start | bytes 18440 | tf_op jit(solution)/shard_map/ppermute | solution.py:434
  299.2 7.0 %collective-permute-done.28 = bf16[192,384]{1,0:T(8,128)(2,1)S(1)} collective-permute-done((bf16[192,384]{1,0:T(8,128)(2,1)S(1)}, bf16[192,384]{1,0:T(8,128)(2,1)S(1)}, u32[]{:S(2)}, u32[]{:S(2)}) %collective-permute-start.28) | collective-permute-done | bytes 147488 | tf_op jit(solution)/shard_map/ppermute | solution.py:431
  306.5 5.0 %collective-permute-done.36 = bf16[192,384]{1,0:T(8,128)(2,1)S(1)} collective-permute-done((bf16[192,384]{1,0:T(8,128)(2,1)S(1)}, bf16[192,384]{1,0:T(8,128)(2,1)S(1)}, u32[]{:S(2)}, u32[]{:S(2)}) %collective-permute-start.36) | collective-permute-done | bytes 147488 | tf_op jit(solution)/shard_map/ppermute | solution.py:431
  311.5 2.0 collective-permute-start.29
  313.6 4.5 %collective-permute-done.29 = bf16[192,384]{1,0:T(8,128)(2,1)S(1)} collective-permute-done((bf16[192,384]{1,0:T(8,128)(2,1)S(1)}, bf16[192,384]{1,0:T(8,128)(2,1)S(1)}, u32[]{:S(2)}, u32[]{:S(2)}) %collective-permute-start.29) | collective-permute-done | bytes 147488 | tf_op jit(solution)/shard_map/ppermute | solution.py:434
  318.3 2.1 collective-permute-start.31
  320.4 2.1 collective-permute-done.50
  325.2 1.8 collective-permute-start.34
  333.5 1.8 collective-permute-start.38
  336.2 3.7 collective-permute-done.43
  340.0 2.4 collective-permute-start.40
  345.8 2.6 collective-permute-done.51
  350.5 2.4 collective-permute-start.54
  354.0 2.3 collective-permute-start.46
  356.3 2.7 collective-permute-start.47
  360.2 1.8 collective-permute-done.47
  362.4 1.8 collective-permute-start.65
  365.8 2.1 collective-permute-start.58
  369.1 13.1 %collective-permute-done.58 = bf16[192,1536]{1,0:T(8,128)(2,1)S(1)} collective-permute-done((bf16[192,1536]{1,0:T(8,128)(2,1)S(1)}, bf16[192,1536]{1,0:T(8,128)(2,1)S(1)}, u32[]{:S(2)}, u32[]{:S(2)}) %collective-permute-start.58) | collective-permute-done | bytes 589856 | tf_op jit(solution)/shard_map/ppermute | solution.py:431
  383.7 7.7 %collective-permute-done.65 = bf16[384,1536]{1,0:T(8,128)(2,1)S(1)} collective-permute-done((bf16[384,1536]{1,0:T(8,128)(2,1)S(1)}, bf16[384,1536]{1,0:T(8,128)(2,1)S(1)}, u32[]{:S(2)}, u32[]{:S(2)}) %collective-permute-start.65) | collective-permute-done | bytes 1179680 | tf_op jit(solution)/shard_map/ppermute | solution.py:434
  391.9 2.1 collective-permute-start.66
  394.2 7.1 %collective-permute-done.59 = bf16[192,1536]{1,0:T(8,128)(2,1)S(1)} collective-permute-done((bf16[192,1536]{1,0:T(8,128)(2,1)S(1)}, bf16[192,1536]{1,0:T(8,128)(2,1)S(1)}, u32[]{:S(2)}, u32[]{:S(2)}) %collective-permute-start.59) | collective-permute-done | bytes 589856 | tf_op jit(solution)/shard_map/ppermute | solution.py:434
  403.2 2.7 collective-permute-start.62
  407.9 4.4 %collective-permute-done.60 = bf16[48,1536]{1,0:T(8,128)(2,1)S(1)} collective-permute-done((bf16[48,1536]{1,0:T(8,128)(2,1)S(1)}, bf16[48,1536]{1,0:T(8,128)(2,1)S(1)}, u32[]{:S(2)}, u32[]{:S(2)}) %collective-permute-start.60) | collective-permute-done | bytes 147488 | tf_op jit(solution)/shard_map/ppermute | solution.py:431
  412.3 1.8 collective-permute-start.69
  416.3 10.4 %collective-permute-done.67 = bf16[48,1536]{1,0:T(8,128)(2,1)S(1)} collective-permute-done((bf16[48,1536]{1,0:T(8,128)(2,1)S(1)}, bf16[48,1536]{1,0:T(8,128)(2,1)S(1)}, u32[]{:S(2)}, u32[]{:S(2)}) %collective-permute-start.67) | collective-permute-done | bytes 147488 | tf_op jit(solution)/shard_map/ppermute | solution.py:431
  (275 shorter events, 78.6 us)
Async XLA Ops:
  5.2 14.3 %collective-permute-start = (bf16[192,1152]{1,0:T(8,128)(2,1)}, bf16[192,1152]{1,0:T(8,128)(2,1)}, u32[]{:S(2)}, u32[]{:S(2)}) collective-permute-start(bf16[192,1152]{1,0:T(8,128)(2,1)} %constant_dynamic-slice_fusion.5), channel_id=1, source_target_pairs={{0,1},{1,0},{2,3},{3,2},{4,5},{5,4},{6,7},{7,6},{8,9},{9,8},{10,11... | collective-permute-start | bytes 1327112 | tf_op jit(solution)/shard_map/ppermute | solution.py:434
  10.1 22.0 %collective-permute-start.10 = (bf16[192,1536]{1,0:T(8,128)(2,1)}, bf16[192,1536]{1,0:T(8,128)(2,1)}, u32[]{:S(2)}, u32[]{:S(2)}) collective-permute-start(bf16[192,1536]{1,0:T(8,128)(2,1)} %constant_dynamic-slice_fusion.3), channel_id=1, source_target_pairs={{0,1},{1,0},{2,3},{3,2},{4,5},{5,4},{6,7},{7,6},{8,9},{9,8},{10,11... | collective-permute-start | bytes 1769480 | tf_op jit(solution)/shard_map/ppermute | solution.py:434
  12.0 31.9 %collective-permute-start.14 = (bf16[384,768]{1,0:T(8,128)(2,1)}, bf16[384,768]{1,0:T(8,128)(2,1)}, u32[]{:S(2)}, u32[]{:S(2)}) collective-permute-start(bf16[384,768]{1,0:T(8,128)(2,1)} %constant_dynamic-slice_fusion.2), channel_id=1, source_target_pairs={{0,1},{1,0},{2,3},{3,2},{4,5},{5,4},{6,7},{7,6},{8,9},{9,8},{10,11... | collective-permute-start | bytes 1769480 | tf_op jit(solution)/shard_map/ppermute | solution.py:434
  19.5 43.8 %collective-permute-start.2 = (bf16[192,1152]{1,0:T(8,128)(2,1)}, bf16[192,1152]{1,0:T(8,128)(2,1)S(1)}, u32[]{:S(2)}, u32[]{:S(2)}) collective-permute-start(bf16[192,1152]{1,0:T(8,128)(2,1)} %collective-permute-done.a), channel_id=1, source_target_pairs={{0,4},{2,6},{4,0},{6,2},{8,12},{10,14},{12,8},{14,10},{16,20},{18,... | collective-permute-start | bytes 1327112 | tf_op jit(solution)/shard_map/ppermute | solution.py:431
  32.1 44.6 %collective-permute-start.12 = (bf16[192,1536]{1,0:T(8,128)(2,1)}, bf16[192,1536]{1,0:T(8,128)(2,1)S(1)}, u32[]{:S(2)}, u32[]{:S(2)}) collective-permute-start(bf16[192,1536]{1,0:T(8,128)(2,1)} %collective-permute-done.10.a), channel_id=1, source_target_pairs={{0,4},{2,6},{4,0},{6,2},{8,12},{10,14},{12,8},{14,10},{16,20},{18,... | collective-permute-start | bytes 1769480 | tf_op jit(solution)/shard_map/ppermute | solution.py:431
  43.9 32.9 %collective-permute-start.16 = (bf16[384,768]{1,0:T(8,128)(2,1)}, bf16[384,768]{1,0:T(8,128)(2,1)S(1)}, u32[]{:S(2)}, u32[]{:S(2)}) collective-permute-start(bf16[384,768]{1,0:T(8,128)(2,1)} %collective-permute-done.14.a), channel_id=1, source_target_pairs={{0,4},{2,6},{4,0},{6,2},{8,12},{10,14},{12,8},{14,10},{16,20},{18,... | collective-permute-start | bytes 1769480 | tf_op jit(solution)/shard_map/ppermute | solution.py:431
  61.1 4.8 %collective-permute-start.5 = (f32[192,128]{1,0:T(8,128)S(1)}, f32[192,128]{1,0:T(8,128)S(1)}, u32[]{:S(2)}, u32[]{:S(2)}) collective-permute-start(f32[192,128]{1,0:T(8,128)S(1)} %dynamic-slice_bitcast_fusion.2), channel_id=1, source_target_pairs={{0,1},{1,0},{2,3},{3,2},{4,5},{5,4},{6,7},{7,6},{8,9},{9,8},{10,11... | collective-permute-start | bytes 294920 | tf_op jit(solution)/shard_map/ppermute | solution.py:434
  63.3 12.9 %collective-permute-start.1 = (bf16[192,1152]{1,0:T(8,128)(2,1)}, bf16[192,1152]{1,0:T(8,128)(2,1)S(1)}, u32[]{:S(2)}, u32[]{:S(2)}) collective-permute-start(bf16[192,1152]{1,0:T(8,128)(2,1)} %collective-permute-done.a), channel_id=1, source_target_pairs={{0,2},{2,0},{4,6},{6,4},{8,10},{10,8},{12,14},{14,12},{16,18},{18,... | collective-permute-start | bytes 1327112 | tf_op jit(solution)/shard_map/ppermute | solution.py:431
  63.3 14.0 %collective-permute-start.3 = (bf16[192,1152]{1,0:T(8,128)(2,1)S(1)}, bf16[192,1152]{1,0:T(8,128)(2,1)S(1)}, u32[]{:S(2)}, u32[]{:S(2)}) collective-permute-start(bf16[192,1152]{1,0:T(8,128)(2,1)S(1)} %collective-permute-done.2.c), channel_id=1, source_target_pairs={{0,2},{2,0},{4,6},{6,4},{8,10},{10,8},{12,14},{14,12},{16,18},{18,... | collective-permute-start | bytes 1327112 | tf_op jit(solution)/shard_map/ppermute | solution.py:431
  65.9 5.1 %collective-permute-start.6 = (bf16[96,768]{1,0:T(8,128)(2,1)S(1)}, bf16[96,768]{1,0:T(8,128)(2,1)S(1)}, u32[]{:S(2)}, u32[]{:S(2)}) collective-permute-start(bf16[96,768]{1,0:T(8,128)(2,1)S(1)} %constant_dynamic-slice_fusion.4), channel_id=1, source_target_pairs={{0,1},{1,0},{2,3},{3,2},{4,5},{5,4},{6,7},{7,6},{8,9},{9,8},{10,11... | collective-permute-start | bytes 442376 | tf_op jit(solution)/shard_map/ppermute | solution.py:434
  71.0 5.1 %collective-permute-start.8 = (bf16[96,768]{1,0:T(8,128)(2,1)S(1)}, bf16[96,768]{1,0:T(8,128)(2,1)S(1)}, u32[]{:S(2)}, u32[]{:S(2)}) collective-permute-start(bf16[96,768]{1,0:T(8,128)(2,1)S(1)} %collective-permute-done.6.a), channel_id=1, source_target_pairs={{0,4},{2,6},{4,0},{6,2},{8,12},{10,14},{12,8},{14,10},{16,20},{18,... | collective-permute-start | bytes 442376 | tf_op jit(solution)/shard_map/ppermute | solution.py:431
  76.2 5.8 %collective-permute-start.7 = (bf16[96,768]{1,0:T(8,128)(2,1)S(1)}, bf16[96,768]{1,0:T(8,128)(2,1)S(1)}, u32[]{:S(2)}, u32[]{:S(2)}) collective-permute-start(bf16[96,768]{1,0:T(8,128)(2,1)S(1)} %collective-permute-done.6.a), channel_id=1, source_target_pairs={{0,2},{2,0},{4,6},{6,4},{8,10},{10,8},{12,14},{14,12},{16,18},{18,... | collective-permute-start | bytes 442376 | tf_op jit(solution)/shard_map/ppermute | solution.py:431
  76.2 44.4 %collective-permute-start.11 = (bf16[192,1536]{1,0:T(8,128)(2,1)}, bf16[192,1536]{1,0:T(8,128)(2,1)S(1)}, u32[]{:S(2)}, u32[]{:S(2)}) collective-permute-start(bf16[192,1536]{1,0:T(8,128)(2,1)} %collective-permute-done.10.a), channel_id=1, source_target_pairs={{0,2},{2,0},{4,6},{6,4},{8,10},{10,8},{12,14},{14,12},{16,18},{18,... | collective-permute-start | bytes 1769480 | tf_op jit(solution)/shard_map/ppermute | solution.py:431
  76.8 43.8 %collective-permute-start.13 = (bf16[192,1536]{1,0:T(8,128)(2,1)S(1)}, bf16[192,1536]{1,0:T(8,128)(2,1)S(1)}, u32[]{:S(2)}, u32[]{:S(2)}) collective-permute-start(bf16[192,1536]{1,0:T(8,128)(2,1)S(1)} %collective-permute-done.12.c), channel_id=1, source_target_pairs={{0,2},{2,0},{4,6},{6,4},{8,10},{10,8},{12,14},{14,12},{16,18},{18,... | collective-permute-start | bytes 1769480 | tf_op jit(solution)/shard_map/ppermute | solution.py:431
  76.9 49.6 %collective-permute-start.15 = (bf16[384,768]{1,0:T(8,128)(2,1)}, bf16[384,768]{1,0:T(8,128)(2,1)S(1)}, u32[]{:S(2)}, u32[]{:S(2)}) collective-permute-start(bf16[384,768]{1,0:T(8,128)(2,1)} %collective-permute-done.14.a), channel_id=1, source_target_pairs={{0,2},{2,0},{4,6},{6,4},{8,10},{10,8},{12,14},{14,12},{16,18},{18,... | collective-permute-start | bytes 1769480 | tf_op jit(solution)/shard_map/ppermute | solution.py:431
  77.3 49.2 %collective-permute-start.17 = (bf16[384,768]{1,0:T(8,128)(2,1)S(1)}, bf16[384,768]{1,0:T(8,128)(2,1)S(1)}, u32[]{:S(2)}, u32[]{:S(2)}) collective-permute-start(bf16[384,768]{1,0:T(8,128)(2,1)S(1)} %collective-permute-done.16.c), channel_id=1, source_target_pairs={{0,2},{2,0},{4,6},{6,4},{8,10},{10,8},{12,14},{14,12},{16,18},{18,... | collective-permute-start | bytes 1769480 | tf_op jit(solution)/shard_map/ppermute | solution.py:431
  82.0 13.3 %collective-permute-start.9 = (bf16[96,768]{1,0:T(8,128)(2,1)S(1)}, bf16[96,768]{1,0:T(8,128)(2,1)S(1)}, u32[]{:S(2)}, u32[]{:S(2)}) collective-permute-start(bf16[96,768]{1,0:T(8,128)(2,1)S(1)} %collective-permute-done.8.c), channel_id=1, source_target_pairs={{0,2},{2,0},{4,6},{6,4},{8,10},{10,8},{12,14},{14,12},{16,18},{18,... | collective-permute-start | bytes 442376 | tf_op jit(solution)/shard_map/ppermute | solution.py:431
  95.9 12.2 %collective-permute-start.4 = (f32[192,128]{1,0:T(8,128)}, f32[192,128]{1,0:T(8,128)}, u32[]{:S(2)}, u32[]{:S(2)}) collective-permute-start(f32[192,128]{1,0:T(8,128)} %dynamic-slice_bitcast_fusion.3), channel_id=1, source_target_pairs={{0,1},{1,0},{2,3},{3,2},{4,5},{5,4},{6,7},{7,6},{8,9},{9,8},{10,11... | collective-permute-start | bytes 294920 | tf_op jit(solution)/shard_map/ppermute | solution.py:434
  164.3 197.8 %collective-permute-start.64 = (bf16[384,1536]{1,0:T(8,128)(2,1)}, bf16[384,1536]{1,0:T(8,128)(2,1)S(1)}, u32[]{:S(2)}, u32[]{:S(2)}) collective-permute-start(bf16[384,1536]{1,0:T(8,128)(2,1)} %slice.288), channel_id=1, source_target_pairs={{0,2},{2,0},{4,6},{6,4},{8,10},{10,8},{12,14},{14,12},{16,18},{18,... | collective-permute-start | bytes 3538952 | tf_op jit(solution)/shard_map/ppermute | solution.py:431
  199.8 164.4 %collective-permute-start.57 = (bf16[384,1536]{1,0:T(8,128)(2,1)}, bf16[384,1536]{1,0:T(8,128)(2,1)}, u32[]{:S(2)}, u32[]{:S(2)}) collective-permute-start(bf16[384,1536]{1,0:T(8,128)(2,1)} %slice.278), channel_id=1, source_target_pairs={{0,2},{2,0},{4,6},{6,4},{8,10},{10,8},{12,14},{14,12},{16,18},{18,... | collective-permute-start | bytes 3538952 | tf_op jit(solution)/shard_map/ppermute | solution.py:431
  231.2 12.1 %collective-permute-start.19 = (f32[192,128]{1,0:T(8,128)}, f32[192,128]{1,0:T(8,128)}, u32[]{:S(2)}, u32[]{:S(2)}) collective-permute-start(f32[192,128]{1,0:T(8,128)} %dynamic-slice_bitcast_fusion), channel_id=1, source_target_pairs={{0,1},{1,0},{2,3},{3,2},{4,5},{5,4},{6,7},{7,6},{8,9},{9,8},{10,11... | collective-permute-start | bytes 294920 | tf_op jit(solution)/shard_map/ppermute | solution.py:434
  240.0 5.0 %collective-permute-start.18 = (f32[192,128]{1,0:T(8,128)}, f32[192,128]{1,0:T(8,128)}, u32[]{:S(2)}, u32[]{:S(2)}) collective-permute-start(f32[192,128]{1,0:T(8,128)} %dynamic-slice_bitcast_fusion.1), channel_id=1, source_target_pairs={{0,1},{1,0},{2,3},{3,2},{4,5},{5,4},{6,7},{7,6},{8,9},{9,8},{10,11... | collective-permute-start | bytes 294920 | tf_op jit(solution)/shard_map/ppermute | solution.py:434
  242.5 75.8 %collective-permute-start.48 = (bf16[384,384]{1,0:T(8,128)(2,1)}, bf16[384,384]{1,0:T(8,128)(2,1)}, u32[]{:S(2)}, u32[]{:S(2)}) collective-permute-start(bf16[384,384]{1,0:T(8,128)(2,1)} %slice.332), channel_id=1, source_target_pairs={{0,2},{2,0},{4,6},{6,4},{8,10},{10,8},{12,14},{14,12},{16,18},{18,... | collective-permute-start | bytes 884744 | tf_op jit(solution)/shard_map/ppermute | solution.py:431
  272.2 21.3 %collective-permute-start.49 = (bf16[384,384]{1,0:T(8,128)(2,1)S(1)}, bf16[384,384]{1,0:T(8,128)(2,1)S(1)}, u32[]{:S(2)}, u32[]{:S(2)}) collective-permute-start(bf16[384,384]{1,0:T(8,128)(2,1)S(1)} %slice.334), channel_id=1, source_target_pairs={{0,2},{2,0},{4,6},{6,4},{8,10},{10,8},{12,14},{14,12},{16,18},{18,... | collective-permute-start | bytes 884744 | tf_op jit(solution)/shard_map/ppermute | solution.py:431
  272.9 3.7 collective-permute-start.21
  276.6 5.1 %collective-permute-start.22 = (f32[2,768]{1,0:T(2,128)S(1)}, f32[2,768]{1,0:T(2,128)S(1)}, u32[]{:S(2)}, u32[]{:S(2)}) collective-permute-start(f32[2,768]{1,0:T(2,128)S(1)} %fusion.28), channel_id=1, source_target_pairs={{0,8},{2,10},{4,12},{6,14},{8,0},{10,2},{12,4},{14,6},{16,24},{18,... | collective-permute-start | bytes 18440 | tf_op jit(solution)/shard_map/ppermute | solution.py:431
  281.7 4.6 %collective-permute-start.23 = (f32[2,768]{1,0:T(2,128)S(1)}, f32[2,768]{1,0:T(2,128)S(1)}, u32[]{:S(2)}, u32[]{:S(2)}) collective-permute-start(f32[2,768]{1,0:T(2,128)S(1)} %add.201), channel_id=1, source_target_pairs={{0,16},{2,18},{4,20},{6,22},{8,24},{10,26},{12,28},{14,30},{16,0},... | collective-permute-start | bytes 18440 | tf_op jit(solution)/shard_map/ppermute | solution.py:431
  286.3 6.7 %collective-permute-start.24 = (f32[2,768]{1,0:T(2,128)S(1)}, f32[2,768]{1,0:T(2,128)S(1)}, u32[]{:S(2)}, u32[]{:S(2)}) collective-permute-start(f32[2,768]{1,0:T(2,128)S(1)} %add.202), channel_id=1, source_target_pairs={{0,1},{1,0},{2,3},{3,2},{4,5},{5,4},{6,7},{7,6},{8,9},{9,8},{10,11... | collective-permute-start | bytes 18440 | tf_op jit(solution)/shard_map/ppermute | solution.py:434
  296.9 16.7 %collective-permute-start.26 = (bf16[192,384]{1,0:T(8,128)(2,1)S(1)}, bf16[192,384]{1,0:T(8,128)(2,1)S(1)}, u32[]{:S(2)}, u32[]{:S(2)}) collective-permute-start(bf16[192,384]{1,0:T(8,128)(2,1)S(1)} %slice.300), channel_id=1, source_target_pairs={{0,4},{2,6},{4,0},{6,2},{8,12},{10,14},{12,8},{14,10},{16,20},{18,... | collective-permute-start | bytes 442376 | tf_op jit(solution)/shard_map/ppermute | solution.py:431
  297.7 8.4 %collective-permute-start.28 = (bf16[192,384]{1,0:T(8,128)(2,1)S(1)}, bf16[192,384]{1,0:T(8,128)(2,1)S(1)}, u32[]{:S(2)}, u32[]{:S(2)}) collective-permute-start(bf16[192,384]{1,0:T(8,128)(2,1)S(1)} %slice.304), channel_id=1, source_target_pairs={{0,4},{2,6},{4,0},{6,2},{8,12},{10,14},{12,8},{14,10},{16,20},{18,... | collective-permute-start | bytes 442376 | tf_op jit(solution)/shard_map/ppermute | solution.py:431
  306.2 5.3 %collective-permute-start.36 = (bf16[192,384]{1,0:T(8,128)(2,1)S(1)}, bf16[192,384]{1,0:T(8,128)(2,1)S(1)}, u32[]{:S(2)}, u32[]{:S(2)}) collective-permute-start(bf16[192,384]{1,0:T(8,128)(2,1)S(1)} %slice.316), channel_id=1, source_target_pairs={{0,4},{2,6},{4,0},{6,2},{8,12},{10,14},{12,8},{14,10},{16,20},{18,... | collective-permute-start | bytes 442376 | tf_op jit(solution)/shard_map/ppermute | solution.py:431
  311.5 6.6 %collective-permute-start.29 = (bf16[192,384]{1,0:T(8,128)(2,1)S(1)}, bf16[192,384]{1,0:T(8,128)(2,1)S(1)}, u32[]{:S(2)}, u32[]{:S(2)}) collective-permute-start(bf16[192,384]{1,0:T(8,128)(2,1)S(1)} %add_convert_fusion.25), channel_id=1, source_target_pairs={{0,1},{1,0},{2,3},{3,2},{4,5},{5,4},{6,7},{7,6},{8,9},{9,8},{10,11... | collective-permute-start | bytes 442376 | tf_op jit(solution)/shard_map/ppermute | solution.py:434
  313.6 8.9 %collective-permute-start.50 = (bf16[384,384]{1,0:T(8,128)(2,1)S(1)}, bf16[384,384]{1,0:T(8,128)(2,1)S(1)}, u32[]{:S(2)}, u32[]{:S(2)}) collective-permute-start(bf16[384,384]{1,0:T(8,128)(2,1)S(1)} %add_convert_fusion.10), channel_id=1, source_target_pairs={{0,1},{1,0},{2,3},{3,2},{4,5},{5,4},{6,7},{7,6},{8,9},{9,8},{10,11... | collective-permute-start | bytes 884744 | tf_op jit(solution)/shard_map/ppermute | solution.py:434
  318.2 6.8 %collective-permute-start.30 = (bf16[48,384]{1,0:T(8,128)(2,1)S(1)}, bf16[48,384]{1,0:T(8,128)(2,1)S(1)}, u32[]{:S(2)}, u32[]{:S(2)}) collective-permute-start(bf16[48,384]{1,0:T(8,128)(2,1)S(1)} %get-tuple-element.95), channel_id=1, source_target_pairs={{0,16},{2,18},{4,20},{6,22},{8,24},{10,26},{12,28},{14,30},{16,0},... | collective-permute-start | bytes 110600 | tf_op jit(solution)/shard_map/ppermute | solution.py:431
  318.3 6.8 %collective-permute-start.31 = (bf16[48,384]{1,0:T(8,128)(2,1)S(1)}, bf16[48,384]{1,0:T(8,128)(2,1)S(1)}, u32[]{:S(2)}, u32[]{:S(2)}) collective-permute-start(bf16[48,384]{1,0:T(8,128)(2,1)S(1)} %get-tuple-element.97), channel_id=1, source_target_pairs={{0,8},{2,10},{4,12},{6,14},{8,0},{10,2},{12,4},{14,6},{16,24},{18,... | collective-permute-start | bytes 110600 | tf_op jit(solution)/shard_map/ppermute | solution.py:431
  322.5 5.8 %collective-permute-start.32 = (bf16[48,384]{1,0:T(8,128)(2,1)S(1)}, bf16[48,384]{1,0:T(8,128)(2,1)S(1)}, u32[]{:S(2)}, u32[]{:S(2)}) collective-permute-start(bf16[48,384]{1,0:T(8,128)(2,1)S(1)} %get-tuple-element.96), channel_id=1, source_target_pairs={{0,24},{2,26},{4,28},{6,30},{8,16},{10,18},{12,20},{14,22},{16,8},... | collective-permute-start | bytes 110600 | tf_op jit(solution)/shard_map/ppermute | solution.py:431
  325.1 10.3 %collective-permute-start.41 = (bf16[384,384]{1,0:T(8,128)(2,1)S(1)}, bf16[384,384]{1,0:T(8,128)(2,1)S(1)}, u32[]{:S(2)}, u32[]{:S(2)}) collective-permute-start(bf16[384,384]{1,0:T(8,128)(2,1)S(1)} %slice.322), channel_id=1, source_target_pairs={{0,2},{2,0},{4,6},{6,4},{8,10},{10,8},{12,14},{14,12},{16,18},{18,... | collective-permute-start | bytes 884744 | tf_op jit(solution)/shard_map/ppermute | solution.py:431
  325.2 6.3 %collective-permute-start.34 = (bf16[192,384]{1,0:T(8,128)(2,1)S(1)}, bf16[192,384]{1,0:T(8,128)(2,1)S(1)}, u32[]{:S(2)}, u32[]{:S(2)}) collective-permute-start(bf16[192,384]{1,0:T(8,128)(2,1)S(1)} %slice.312), channel_id=1, source_target_pairs={{0,4},{2,6},{4,0},{6,2},{8,12},{10,14},{12,8},{14,10},{16,20},{18,... | collective-permute-start | bytes 442376 | tf_op jit(solution)/shard_map/ppermute | solution.py:431
  328.3 5.1 %collective-permute-start.37 = (bf16[192,384]{1,0:T(8,128)(2,1)S(1)}, bf16[192,384]{1,0:T(8,128)(2,1)S(1)}, u32[]{:S(2)}, u32[]{:S(2)}) collective-permute-start(bf16[192,384]{1,0:T(8,128)(2,1)S(1)} %add_convert_fusion.22), channel_id=1, source_target_pairs={{0,1},{1,0},{2,3},{3,2},{4,5},{5,4},{6,7},{7,6},{8,9},{9,8},{10,11... | collective-permute-start | bytes 442376 | tf_op jit(solution)/shard_map/ppermute | solution.py:434
  331.4 8.6 %collective-permute-start.43 = (bf16[384,384]{1,0:T(8,128)(2,1)S(1)}, bf16[384,384]{1,0:T(8,128)(2,1)S(1)}, u32[]{:S(2)}, u32[]{:S(2)}) collective-permute-start(bf16[384,384]{1,0:T(8,128)(2,1)S(1)} %add_convert_fusion.13), channel_id=1, source_target_pairs={{0,1},{1,0},{2,3},{3,2},{4,5},{5,4},{6,7},{7,6},{8,9},{9,8},{10,11... | collective-permute-start | bytes 884744 | tf_op jit(solution)/shard_map/ppermute | solution.py:434
  333.5 9.0 %collective-permute-start.38 = (bf16[48,384]{1,0:T(8,128)(2,1)S(1)}, bf16[48,384]{1,0:T(8,128)(2,1)S(1)}, u32[]{:S(2)}, u32[]{:S(2)}) collective-permute-start(bf16[48,384]{1,0:T(8,128)(2,1)S(1)} %get-tuple-element.98), channel_id=1, source_target_pairs={{0,16},{2,18},{4,20},{6,22},{8,24},{10,26},{12,28},{14,30},{16,0},... | collective-permute-start | bytes 110600 | tf_op jit(solution)/shard_map/ppermute | solution.py:431
  335.3 8.0 %collective-permute-start.39 = (bf16[48,384]{1,0:T(8,128)(2,1)S(1)}, bf16[48,384]{1,0:T(8,128)(2,1)S(1)}, u32[]{:S(2)}, u32[]{:S(2)}) collective-permute-start(bf16[48,384]{1,0:T(8,128)(2,1)S(1)} %get-tuple-element.100), channel_id=1, source_target_pairs={{0,8},{2,10},{4,12},{6,14},{8,0},{10,2},{12,4},{14,6},{16,24},{18,... | collective-permute-start | bytes 110600 | tf_op jit(solution)/shard_map/ppermute | solution.py:431
  340.0 5.8 %collective-permute-start.40 = (bf16[48,384]{1,0:T(8,128)(2,1)S(1)}, bf16[48,384]{1,0:T(8,128)(2,1)S(1)}, u32[]{:S(2)}, u32[]{:S(2)}) collective-permute-start(bf16[48,384]{1,0:T(8,128)(2,1)S(1)} %get-tuple-element.99), channel_id=1, source_target_pairs={{0,24},{2,26},{4,28},{6,30},{8,16},{10,18},{12,20},{14,22},{16,8},... | collective-permute-start | bytes 110600 | tf_op jit(solution)/shard_map/ppermute | solution.py:431
  342.5 5.9 %collective-permute-start.51 = (bf16[192,384]{1,0:T(8,128)(2,1)S(1)}, bf16[192,384]{1,0:T(8,128)(2,1)S(1)}, u32[]{:S(2)}, u32[]{:S(2)}) collective-permute-start(bf16[192,384]{1,0:T(8,128)(2,1)S(1)} %slice.336), channel_id=1, source_target_pairs={{0,4},{2,6},{4,0},{6,2},{8,12},{10,14},{12,8},{14,10},{16,20},{18,... | collective-permute-start | bytes 442376 | tf_op jit(solution)/shard_map/ppermute | solution.py:431
  343.3 7.2 %collective-permute-start.44 = (bf16[192,384]{1,0:T(8,128)(2,1)S(1)}, bf16[192,384]{1,0:T(8,128)(2,1)S(1)}, u32[]{:S(2)}, u32[]{:S(2)}) collective-permute-start(bf16[192,384]{1,0:T(8,128)(2,1)S(1)} %slice.326), channel_id=1, source_target_pairs={{0,4},{2,6},{4,0},{6,2},{8,12},{10,14},{12,8},{14,10},{16,20},{18,... | collective-permute-start | bytes 442376 | tf_op jit(solution)/shard_map/ppermute | solution.py:431
  348.4 5.5 %collective-permute-start.52 = (bf16[48,384]{1,0:T(8,128)(2,1)S(1)}, bf16[48,384]{1,0:T(8,128)(2,1)S(1)}, u32[]{:S(2)}, u32[]{:S(2)}) collective-permute-start(bf16[48,384]{1,0:T(8,128)(2,1)S(1)} %get-tuple-element.92), channel_id=1, source_target_pairs={{0,16},{2,18},{4,20},{6,22},{8,24},{10,26},{12,28},{14,30},{16,0},... | collective-permute-start | bytes 110600 | tf_op jit(solution)/shard_map/ppermute | solution.py:431
  348.9 5.1 %collective-permute-start.53 = (bf16[48,384]{1,0:T(8,128)(2,1)S(1)}, bf16[48,384]{1,0:T(8,128)(2,1)S(1)}, u32[]{:S(2)}, u32[]{:S(2)}) collective-permute-start(bf16[48,384]{1,0:T(8,128)(2,1)S(1)} %get-tuple-element.94), channel_id=1, source_target_pairs={{0,8},{2,10},{4,12},{6,14},{8,0},{10,2},{12,4},{14,6},{16,24},{18,... | collective-permute-start | bytes 110600 | tf_op jit(solution)/shard_map/ppermute | solution.py:431
  350.5 5.8 %collective-permute-start.54 = (bf16[48,384]{1,0:T(8,128)(2,1)S(1)}, bf16[48,384]{1,0:T(8,128)(2,1)S(1)}, u32[]{:S(2)}, u32[]{:S(2)}) collective-permute-start(bf16[48,384]{1,0:T(8,128)(2,1)S(1)} %get-tuple-element.93), channel_id=1, source_target_pairs={{0,24},{2,26},{4,28},{6,30},{8,16},{10,18},{12,20},{14,22},{16,8},... | collective-permute-start | bytes 110600 | tf_op jit(solution)/shard_map/ppermute | solution.py:431
  353.9 5.8 %collective-permute-start.45 = (bf16[48,384]{1,0:T(8,128)(2,1)S(1)}, bf16[48,384]{1,0:T(8,128)(2,1)S(1)}, u32[]{:S(2)}, u32[]{:S(2)}) collective-permute-start(bf16[48,384]{1,0:T(8,128)(2,1)S(1)} %get-tuple-element.101), channel_id=1, source_target_pairs={{0,16},{2,18},{4,20},{6,22},{8,24},{10,26},{12,28},{14,30},{16,0},... | collective-permute-start | bytes 110600 | tf_op jit(solution)/shard_map/ppermute | solution.py:431
  354.0 5.7 %collective-permute-start.46 = (bf16[48,384]{1,0:T(8,128)(2,1)S(1)}, bf16[48,384]{1,0:T(8,128)(2,1)S(1)}, u32[]{:S(2)}, u32[]{:S(2)}) collective-permute-start(bf16[48,384]{1,0:T(8,128)(2,1)S(1)} %get-tuple-element.103), channel_id=1, source_target_pairs={{0,8},{2,10},{4,12},{6,14},{8,0},{10,2},{12,4},{14,6},{16,24},{18,... | collective-permute-start | bytes 110600 | tf_op jit(solution)/shard_map/ppermute | solution.py:431
  356.3 5.8 %collective-permute-start.47 = (bf16[48,384]{1,0:T(8,128)(2,1)S(1)}, bf16[48,384]{1,0:T(8,128)(2,1)S(1)}, u32[]{:S(2)}, u32[]{:S(2)}) collective-permute-start(bf16[48,384]{1,0:T(8,128)(2,1)S(1)} %get-tuple-element.102), channel_id=1, source_target_pairs={{0,24},{2,26},{4,28},{6,30},{8,16},{10,18},{12,20},{14,22},{16,8},... | collective-permute-start | bytes 110600 | tf_op jit(solution)/shard_map/ppermute | solution.py:431
  359.7 24.0 %collective-permute-start.63 = (bf16[384,1536]{1,0:T(8,128)(2,1)S(1)}, bf16[384,1536]{1,0:T(8,128)(2,1)S(1)}, u32[]{:S(2)}, u32[]{:S(2)}) collective-permute-start(bf16[384,1536]{1,0:T(8,128)(2,1)S(1)} %copy-done.6), channel_id=1, source_target_pairs={{0,2},{2,0},{4,6},{6,4},{8,10},{10,8},{12,14},{14,12},{16,18},{18,... | collective-permute-start | bytes 3538952 | tf_op jit(solution)/shard_map/ppermute | solution.py:431
  359.7 8.9 %collective-permute-start.55 = (bf16[384,1536]{1,0:T(8,128)(2,1)S(1)}, bf16[384,1536]{1,0:T(8,128)(2,1)S(1)}, u32[]{:S(2)}, u32[]{:S(2)}) collective-permute-start(bf16[384,1536]{1,0:T(8,128)(2,1)S(1)} %copy-done.7), channel_id=1, source_target_pairs={{0,2},{2,0},{4,6},{6,4},{8,10},{10,8},{12,14},{14,12},{16,18},{18,... | collective-permute-start | bytes 3538952 | tf_op jit(solution)/shard_map/ppermute | solution.py:431
  362.4 29.0 %collective-permute-start.65 = (bf16[384,1536]{1,0:T(8,128)(2,1)S(1)}, bf16[384,1536]{1,0:T(8,128)(2,1)S(1)}, u32[]{:S(2)}, u32[]{:S(2)}) collective-permute-start(bf16[384,1536]{1,0:T(8,128)(2,1)S(1)} %add_convert_fusion.1), channel_id=1, source_target_pairs={{0,1},{1,0},{2,3},{3,2},{4,5},{5,4},{6,7},{7,6},{8,9},{9,8},{10,11... | collective-permute-start | bytes 3538952 | tf_op jit(solution)/shard_map/ppermute | solution.py:434
  365.8 16.4 %collective-permute-start.58 = (bf16[192,1536]{1,0:T(8,128)(2,1)S(1)}, bf16[192,1536]{1,0:T(8,128)(2,1)S(1)}, u32[]{:S(2)}, u32[]{:S(2)}) collective-permute-start(bf16[192,1536]{1,0:T(8,128)(2,1)S(1)} %slice.344), channel_id=1, source_target_pairs={{0,4},{2,6},{4,0},{6,2},{8,12},{10,14},{12,8},{14,10},{16,20},{18,... | collective-permute-start | bytes 1769480 | tf_op jit(solution)/shard_map/ppermute | solution.py:431
  369.0 25.2 %collective-permute-start.56 = (bf16[192,1536]{1,0:T(8,128)(2,1)S(1)}, bf16[192,1536]{1,0:T(8,128)(2,1)S(1)}, u32[]{:S(2)}, u32[]{:S(2)}) collective-permute-start(bf16[192,1536]{1,0:T(8,128)(2,1)S(1)} %slice.342), channel_id=1, source_target_pairs={{0,4},{2,6},{4,0},{6,2},{8,12},{10,14},{12,8},{14,10},{16,20},{18,... | collective-permute-start | bytes 1769480 | tf_op jit(solution)/shard_map/ppermute | solution.py:431
  382.3 18.9 %collective-permute-start.59 = (bf16[192,1536]{1,0:T(8,128)(2,1)S(1)}, bf16[192,1536]{1,0:T(8,128)(2,1)S(1)}, u32[]{:S(2)}, u32[]{:S(2)}) collective-permute-start(bf16[192,1536]{1,0:T(8,128)(2,1)S(1)} %add_convert_fusion.7), channel_id=1, source_target_pairs={{0,1},{1,0},{2,3},{3,2},{4,5},{5,4},{6,7},{7,6},{8,9},{9,8},{10,11... | collective-permute-start | bytes 1769480 | tf_op jit(solution)/shard_map/ppermute | solution.py:434
  391.9 14.1 %collective-permute-start.66 = (bf16[192,1536]{1,0:T(8,128)(2,1)S(1)}, bf16[192,1536]{1,0:T(8,128)(2,1)S(1)}, u32[]{:S(2)}, u32[]{:S(2)}) collective-permute-start(bf16[192,1536]{1,0:T(8,128)(2,1)S(1)} %slice.350), channel_id=1, source_target_pairs={{0,4},{2,6},{4,0},{6,2},{8,12},{10,14},{12,8},{14,10},{16,20},{18,... | collective-permute-start | bytes 1769480 | tf_op jit(solution)/shard_map/ppermute | solution.py:431
  401.5 10.8 %collective-permute-start.60 = (bf16[48,1536]{1,0:T(8,128)(2,1)S(1)}, bf16[48,1536]{1,0:T(8,128)(2,1)S(1)}, u32[]{:S(2)}, u32[]{:S(2)}) collective-permute-start(bf16[48,1536]{1,0:T(8,128)(2,1)S(1)} %get-tuple-element.89), channel_id=1, source_target_pairs={{0,16},{2,18},{4,20},{6,22},{8,24},{10,26},{12,28},{14,30},{16,0},... | collective-permute-start | bytes 442376 | tf_op jit(solution)/shard_map/ppermute | solution.py:431
  402.5 11.6 %collective-permute-start.61 = (bf16[48,1536]{1,0:T(8,128)(2,1)S(1)}, bf16[48,1536]{1,0:T(8,128)(2,1)S(1)}, u32[]{:S(2)}, u32[]{:S(2)}) collective-permute-start(bf16[48,1536]{1,0:T(8,128)(2,1)S(1)} %get-tuple-element.91), channel_id=1, source_target_pairs={{0,8},{2,10},{4,12},{6,14},{8,0},{10,2},{12,4},{14,6},{16,24},{18,... | collective-permute-start | bytes 442376 | tf_op jit(solution)/shard_map/ppermute | solution.py:431
  403.2 12.3 %collective-permute-start.62 = (bf16[48,1536]{1,0:T(8,128)(2,1)S(1)}, bf16[48,1536]{1,0:T(8,128)(2,1)S(1)}, u32[]{:S(2)}, u32[]{:S(2)}) collective-permute-start(bf16[48,1536]{1,0:T(8,128)(2,1)S(1)} %get-tuple-element.90), channel_id=1, source_target_pairs={{0,24},{2,26},{4,28},{6,30},{8,16},{10,18},{12,20},{14,22},{16,8},... | collective-permute-start | bytes 442376 | tf_op jit(solution)/shard_map/ppermute | solution.py:431
  406.2 20.6 %collective-permute-start.67 = (bf16[48,1536]{1,0:T(8,128)(2,1)S(1)}, bf16[48,1536]{1,0:T(8,128)(2,1)S(1)}, u32[]{:S(2)}, u32[]{:S(2)}) collective-permute-start(bf16[48,1536]{1,0:T(8,128)(2,1)S(1)} %get-tuple-element.86), channel_id=1, source_target_pairs={{0,16},{2,18},{4,20},{6,22},{8,24},{10,26},{12,28},{14,30},{16,0},... | collective-permute-start | bytes 442376 | tf_op jit(solution)/shard_map/ppermute | solution.py:431
  406.3 20.4 %collective-permute-start.68 = (bf16[48,1536]{1,0:T(8,128)(2,1)S(1)}, bf16[48,1536]{1,0:T(8,128)(2,1)S(1)}, u32[]{:S(2)}, u32[]{:S(2)}) collective-permute-start(bf16[48,1536]{1,0:T(8,128)(2,1)S(1)} %get-tuple-element.88), channel_id=1, source_target_pairs={{0,8},{2,10},{4,12},{6,14},{8,0},{10,2},{12,4},{14,6},{16,24},{18,... | collective-permute-start | bytes 442376 | tf_op jit(solution)/shard_map/ppermute | solution.py:431
  412.3 14.4 %collective-permute-start.69 = (bf16[48,1536]{1,0:T(8,128)(2,1)S(1)}, bf16[48,1536]{1,0:T(8,128)(2,1)S(1)}, u32[]{:S(2)}, u32[]{:S(2)}) collective-permute-start(bf16[48,1536]{1,0:T(8,128)(2,1)S(1)} %get-tuple-element.87), channel_id=1, source_target_pairs={{0,24},{2,26},{4,28},{6,30},{8,16},{10,18},{12,20},{14,22},{16,8},... | collective-permute-start | bytes 442376 | tf_op jit(solution)/shard_map/ppermute | solution.py:431
  (47 other events, 412.8 us)
